TPU v7x, 32 devices: a whole 2x2x4 slice. The times are simulated.
32 devices in a mesh: dp: 4 (over z), fsdp: 8 (over y, x, core).
Axes of the slice: x: 2, y: 2, z: 4, core: 2. Of those that a mesh axis runs over, the one named last changes fastest.
Arguments:
- qkv: bfloat16 [4, 8, 192, 3, 896], P('dp', 'fsdp'), may hold values from -8 to 8
- grad_out: bfloat16 [4, 8, 192, 896], P('dp', 'fsdp'), may hold values from -6 to 6
- lengths: int32 [4, 8, 3], P(None, 'fsdp'), may hold values from 1 to 128, 192 in all within a row
- moves: int32 [8, 2, 3], P('fsdp'), may hold values from 0 to 3, as said below
- out_weight: bfloat16 [896, 896], P('fsdp'), may hold values from -0.1875 to 0.1875
Outputs:
- home_grad: bfloat16 [4, 8, 192, 3, 896], P('dp', 'fsdp')
- inbox_grad: bfloat16 [4, 8, 128, 3, 896], P('dp', 'fsdp')
- weight_grad: float32 [896, 896], P('fsdp', 'dp')
Inputs may be any that keep to these rules, and one draw needn't show every extreme that they name: In each fsdp column the sources of the moves differ from one another, and each destination is (source + 1) mod 4; the clip index is below 3. `lengths`: each device's counts sum to 192.
All inputs are finite; a program needn't handle non-finite values.
Results may differ from a plain program's by a relative error of at most 0.023.
Values may be sent and summed in bfloat16 or wider, within the bound.
A program may use at most 64 MiB of HBM per device.

v0:
```python
import jax
import jax.numpy as jnp
from jax import lax
from jax.sharding import PartitionSpec as P

HEADS = 8
HSIZE = 112
TOK_DEV = 192
CLIP_MAX = 128


def passed_along(shard, axis, by):
    length = lax.axis_size(axis)
    return lax.ppermute(shard, axis, [(i, (i + by) % length) for i in range(length)])


def attend(rows, allowed, live):
    length = rows.shape[0]
    split = rows.reshape(length, 3, HEADS, HSIZE)
    queries = split[:, 0]
    keys = split[:, 1]
    values = split[:, 2]
    scores = jnp.einsum(
        "qhd,khd->hqk", queries, keys, preferred_element_type=jnp.float32
    ) * HSIZE ** (-0.5)
    scores = jnp.where(allowed[None], scores, -1000000000.0)
    probs = jax.nn.softmax(scores, axis=-1).astype(jnp.bfloat16)
    mixed = jnp.einsum("hqk,khd->qhd", probs, values, preferred_element_type=jnp.float32)
    mixed = jnp.where(live[:, None, None], mixed, 0.0)
    return mixed.reshape(length, HEADS * HSIZE).astype(jnp.bfloat16)


def clip_start(counts, which):
    starts = jnp.cumsum(counts) - counts
    clips = jnp.arange(counts.shape[0], dtype=jnp.int32)
    return (
        jnp.sum(jnp.where(clips == which, starts, 0)),
        jnp.sum(jnp.where(clips == which, counts, 0)),
    )


def home_masks(counts, moving, rank):
    ends = jnp.cumsum(counts)
    places = jnp.arange(TOK_DEV, dtype=jnp.int32)
    segment = jnp.sum((places[:, None] >= ends[None, :]).astype(jnp.int32), axis=1)
    clips = jnp.arange(counts.shape[0], dtype=jnp.int32)
    gone = jnp.any((moving[:, 0:1] == rank) & (moving[:, 2:3] == clips[None, :]), axis=0)
    stays = jnp.logical_not(jnp.any((segment[:, None] == clips[None, :]) & gone[None, :], axis=1))
    return (segment[:, None] == segment[None, :], stays)


def local(qkv, grad_out, lengths, moves, out_weight):
    home_rows = qkv[0, 0]
    home_cot = grad_out[0, 0]
    counts_all = lengths[:, 0]
    moving = moves[0]
    rank = lax.axis_index("dp")
    ranks = jnp.arange(counts_all.shape[0], dtype=jnp.int32)
    counts = jnp.sum(jnp.where((ranks == rank)[:, None], counts_all, 0), axis=0)
    allowed_home, stays = home_masks(counts, moving, rank)
    padded = jnp.concatenate(
        [home_rows, jnp.zeros((CLIP_MAX,) + home_rows.shape[1:], home_rows.dtype)], axis=0
    )
    cot_pad = jnp.concatenate(
        [home_cot, jnp.zeros((CLIP_MAX, home_cot.shape[1]), home_cot.dtype)], axis=0
    )
    send_off = jnp.zeros((), jnp.int32)
    sending = jnp.zeros((), jnp.bool_)
    box_len = jnp.zeros((), jnp.int32)
    receiving = jnp.zeros((), jnp.bool_)
    for step in range(moving.shape[0]):
        source = moving[step, 0]
        which = moving[step, 2]
        mine_out = source == rank
        offset, unused = clip_start(counts, which)
        send_off = jnp.where(mine_out, offset, send_off)
        sending = jnp.logical_or(sending, mine_out)
        source_counts = jnp.sum(jnp.where((ranks == source)[:, None], counts_all, 0), axis=0)
        ignored, length = clip_start(source_counts, which)
        mine_in = moving[step, 1] == rank
        box_len = jnp.where(mine_in, length, box_len)
        receiving = jnp.logical_or(receiving, mine_in)
    out_rows = jnp.where(
        sending,
        lax.dynamic_slice_in_dim(padded, send_off, CLIP_MAX, 0),
        jnp.zeros((), jnp.bfloat16),
    )
    out_cot = jnp.where(
        sending,
        lax.dynamic_slice_in_dim(cot_pad, send_off, CLIP_MAX, 0),
        jnp.zeros((), jnp.bfloat16),
    )
    got_rows, got_cot = passed_along((out_rows, out_cot), "dp", 1)
    box_rows = jnp.where(receiving, got_rows, jnp.zeros((), jnp.bfloat16))
    box_cot = jnp.where(receiving, got_cot, jnp.zeros((), jnp.bfloat16))
    places = jnp.arange(CLIP_MAX, dtype=jnp.int32)
    box_live = places < box_len
    box_allowed = jnp.broadcast_to(box_live[None, :], (CLIP_MAX, CLIP_MAX))

    def forward(home_in, box_in):
        return (attend(home_in, allowed_home, stays), attend(box_in, box_allowed, box_live))

    (mixed_home, mixed_box), pullback = jax.vjp(forward, home_rows, box_rows)
    weights = lax.all_gather(out_weight, "fsdp", axis=0, tiled=True)
    mixed_all = jnp.concatenate([mixed_home, mixed_box], axis=0)
    cot_all = jnp.concatenate([home_cot, box_cot], axis=0)
    back = lax.dot_general(
        cot_all, weights, (((1,), (1,)), ((), ())), preferred_element_type=jnp.float32
    ).astype(jnp.bfloat16)
    tokens_dev = home_rows.shape[0]
    grad_home, grad_box = pullback((back[:tokens_dev], back[tokens_dev:]))
    shard_rows = out_weight.shape[0]
    rank_sum = lax.psum_scatter(
        lax.dot_general(
            cot_all, mixed_all, (((0,), (0,)), ((), ())), preferred_element_type=jnp.float32
        ).astype(jnp.bfloat16),
        "dp",
        scatter_dimension=0,
        tiled=True,
    ).astype(jnp.float32)
    whole = lax.psum(rank_sum, "fsdp")
    piece = lax.dynamic_slice_in_dim(whole, lax.axis_index("fsdp") * shard_rows, shard_rows, 1)
    weight_grad = jnp.transpose(piece)
    return (grad_home[None, None], grad_box[None, None], weight_grad)


def solution(mesh):
    placed = (
        P("dp", "fsdp", None, None, None),
        P("dp", "fsdp", None, None),
        P(None, "fsdp", None),
        P("fsdp", None, None),
        P("fsdp", None),
    )
    return jax.shard_map(
        local,
        mesh=mesh,
        in_specs=placed,
        out_specs=(
            P("dp", "fsdp", None, None, None),
            P("dp", "fsdp", None, None, None),
            P("fsdp", "dp"),
        ),
        check_vma=False,
    )
```

profile of v0, /device:TPU:0, one launch (start us, length us, event | category | flops | bytes accessed | tf_op | source)
XLA Modules:
  0.0 128.3 jit_solution(3870639444129556366)
XLA Ops:
  8.1 0.7 all-gather.2.cloned.1.call-update
  8.8 1.6 %fusion.66 = (s32[1,1]{1,0:T(1,128)}, s32[1,1]{1,0:T(1,128)}, s32[1,1]{1,0:T(1,128)}, s32[1,1]{1,0:T(1,128)}, s32[1,1]{1,0:T(1,128)}, /*index=5*/s32[1,1]{1,0:T(1,128)}) fusion(s32[2,3]{1,0:T(2,128)} %bitcast.145), kind=kLoop, calls=%fused_computation.121 | loop fusion | bytes 48 | tf_op jit(solution)/shard_map/slice | solution.py:80
  10.3 0.7 iota_compare_fusion.3
  11.7 0.6 iota_compare_fusion.2
  13.0 0.8 copy.39
  14.0 2.0 %fusion.49 = (s32[]{:T(128)}, s32[]{:T(128)}, s32[]{:T(128)}) fusion(s32[]{:T(128)} %bitcast.10, s32[3]{0:T(128)S(1)} %get-tuple-element.14, s32[3,1]{0,1:T(1,128)S(1)} %reduce-window.8, s32[]{:T(128)} %bitcast.9, s32[3]{0:T(128)S(1)} %get-tuple-element.13), kind=kLoop, calls=%fused_computation.102 | loop fusion | flops 24 | bytes 56 | tf_op jit(solution)/shard_map/reduce_sum | solution.py:37
  17.3 1.7 %fusion.37 = bf16[128,896]{1,0:T(8,128)(2,1)} fusion(s32[]{:T(128)S(6)} %select_n.112, bf16[192,896]{1,0:T(8,128)(2,1)} %bitcast.141, pred[]{:T(512)S(6)} %or.7), kind=kLoop, calls=%fused_computation.68 | loop fusion | flops 114688 | bytes 573445 | tf_op jit(solution)/shard_map/jit(_where)/select_n | solution.py:88
  19.0 3.0 %collective-permute-start = (bf16[128,896]{1,0:T(8,128)(2,1)}, bf16[128,896]{1,0:T(8,128)(2,1)}, u32[]{:S(2)}, u32[]{:S(2)}) collective-permute-start(bf16[128,896]{1,0:T(8,128)(2,1)} %fusion.37), channel_id=1, source_target_pairs={{0,8},{8,16},{16,24},{24,0},{1,9},{9,17},{17,25},{25,1},{2,10},{10... | collective-permute-start | bytes 688136 | tf_op jit(solution)/shard_map/ppermute | solution.py:14
  22.0 1.2 fusion.25
  23.3 1.7 %collective-permute-start.1 = (bf16[128,3,896]{2,0,1:T(8,128)(2,1)S(1)}, bf16[128,3,896]{2,0,1:T(8,128)(2,1)}, u32[]{:S(2)}, u32[]{:S(2)}) collective-permute-start(bf16[128,3,896]{2,0,1:T(8,128)(2,1)S(1)} %fusion.25), channel_id=1, source_target_pairs={{0,8},{8,16},{16,24},{24,0},{1,9},{9,17},{17,25},{25,1},{2,10},{10... | collective-permute-start | bytes 2064392 | tf_op jit(solution)/shard_map/ppermute | solution.py:14
  25.0 1.4 %reshape_squeeze.3 = bf16[192,3,8,112]{3,2,0,1:T(8,128)(2,1)S(1)} reshape(bf16[1,1,192,3,896]{4,2,3,1,0:T(8,128)(2,1)S(1)} %copy-done) | data formatting | bytes 2064384 | tf_op jit(solution)/shard_map/jvp()/reshape;squeeze | solution.py:19
  27.1 1.0 fusion.65
  28.0 1.8 %fusion.67 = (f32[8,192]{1,0:T(8,128)S(1)}, f32[8,192,192]{1,2,0:T(8,128)S(1)}) fusion(pred[192,192]{0,1:T(8,128)(4,1)S(1)} %broadcast_compare_fusion, bf16[192,1,8,112]{3,2,0,1:T(8,128)(2,1)} %get-tuple-element.19, bf16[192,1,8,112]{3,2,0,1:T(8,128)(2,1)} %get-tuple-element.18), kind=kOutput, calls=%fused_computation.122 | convolution fusion | flops 67240128 | bytes 1910784 | tf_op jit(solution)/shard_map/jvp()/sub | solution.py:27
  29.8 1.3 fusion.16
  32.3 1.3 %fusion.50 = s32[]{:T(128)} fusion(s32[3]{0:T(128)S(1)} %get-tuple-element.12, s32[]{:T(128)} %bitcast.10), kind=kLoop, calls=%fused_computation.103 | loop fusion | flops 8 | bytes 20 | tf_op jit(solution)/shard_map/reduce_sum | solution.py:38
  34.3 1.3 copy.52
  35.5 1.0 convert_element_type.108
  37.2 0.7 broadcast_select_fusion.1
  38.0 6.8 %collective-permute-done.1 = bf16[128,3,896]{2,0,1:T(8,128)(2,1)} collective-permute-done((bf16[128,3,896]{2,0,1:T(8,128)(2,1)S(1)}, bf16[128,3,896]{2,0,1:T(8,128)(2,1)}, u32[]{:S(2)}, u32[]{:S(2)}) %collective-permute-start.1) | collective-permute-done | bytes 688160 | tf_op jit(solution)/shard_map/ppermute | solution.py:14
  45.6 1.0 fusion.19
  46.6 1.1 copy.54
  47.6 3.5 %convolution_convert_fusion = bf16[896,896]{1,0:T(8,128)(2,1)} fusion(bf16[128,896]{1,0:T(8,128)(2,1)S(1)} %copy.54, bf16[192,896]{1,0:T(8,128)(2,1)} %convert_element_type.108, bf16[128,896]{1,0:T(8,128)(2,1)} %broadcast_select_fusion.1, bf16[192,896]{1,0:T(8,128)(2,1)} %bitcast.142), kind=kOutput, calls=%fused_computation.5 | convolution fusion | flops 516898816 | bytes 2752512 | tf_op jit(solution)/shard_map/dot_general | solution.py:114
  51.2 0.9 copy-done.8
  52.1 2.3 %convolution_convert_fusion.2 = bf16[320,896]{1,0:T(8,128)(2,1)S(1)} fusion(bf16[896,896]{1,0:T(8,128)(2,1)} %all-gather.2.cloned.1.call-done, bf16[128,896]{1,0:T(8,128)(2,1)S(1)} %copy-done.9, bf16[192,896]{1,0:T(8,128)(2,1)S(1)} %bitcast.143), kind=kOutput, calls=%fused_computation.17 | convolution fusion | flops 515235840 | bytes 2752512 | tf_op jit(solution)/shard_map/dot_general | solution.py:107
  54.5 0.8 copy-done.3
  57.2 0.7 fusion.15
  59.1 0.8 copy.45
  60.0 1.8 %reshape.128 = bf16[1,1,192,3,896]{4,2,3,1,0:T(8,128)(2,1)} reshape(bf16[192,3,8,112]{3,2,0,1:T(8,128)(2,1)S(1)} %copy.45) | data formatting | bytes 2064384 | tf_op jit(solution)/shard_map/broadcast_in_dim;transpose(jvp())/reshape | solution.py:124
  63.3 1.1 copy.55
  64.4 23.1 %reduce-scatter.2.cloned.1.call-done = bf16[224,896]{1,0:T(8,128)(2,1)} async-done(((bf16[896,896]{1,0:T(8,128)(2,1)}), bf16[224,896]{1,0:T(8,128)(2,1)}) %reduce-scatter.2.cloned.1.call-update) | async-done | bytes 401424 | tf_op jit(solution)/shard_map/reduce_scatter | solution.py:113
  87.5 32.4 %all-reduce.9 = f32[224,896]{1,0:T(8,128)S(1)} all-reduce(bf16[224,896]{1,0:T(8,128)(2,1)} %reduce-scatter.2.cloned.1.call-done), channel_id=1, replica_groups=mesh['dp'=4,'fsdp'=8] {'fsdp'}, use_global_device_ids=true, to_apply=%region_18.19 | all-reduce | flops 200704 | bytes 1204224 | tf_op jit(solution)/shard_map/psum | solution.py:121
  120.1 0.7 copy.56
  (58 shorter events, 6.8 us)
Async XLA Ops:
  8.0 17.0 %copy-start = (bf16[1,1,192,3,896]{4,2,3,1,0:T(8,128)(2,1)S(1)}, bf16[1,1,192,3,896]{4,2,3,1,0:T(8,128)(2,1)}, u32[]{:S(2)}) copy-start(bf16[1,1,192,3,896]{4,2,3,1,0:T(8,128)(2,1)} %param.5) | copy-start | bytes 3096580
  8.0 43.2 %all-gather.2.cloned.1.call-start = ((), (), s32[]{:S(2)}) async-start(), calls=%async_computation.1 | async-start | bytes 1806336 | tf_op jit(solution)/shard_map/all_gather | solution.py:104
  8.7 78.8 %reduce-scatter.2.cloned.1.call-start = ((), (), s32[]{:S(2)}) async-start(), calls=%async_computation.2 | async-start | bytes 2007040 | tf_op jit(solution)/shard_map/reduce_scatter | solution.py:113
  19.0 18.2 %collective-permute-start = (bf16[128,896]{1,0:T(8,128)(2,1)}, bf16[128,896]{1,0:T(8,128)(2,1)}, u32[]{:S(2)}, u32[]{:S(2)}) collective-permute-start(bf16[128,896]{1,0:T(8,128)(2,1)} %fusion.37), channel_id=1, source_target_pairs={{0,8},{8,16},{16,24},{24,0},{1,9},{9,17},{17,25},{25,1},{2,10},{10... | collective-permute-start | bytes 688136 | tf_op jit(solution)/shard_map/ppermute | solution.py:14
  22.0 4.3 %copy-start.10 = (s32[1,2,3]{2,1,0:T(2,128)S(1)}, s32[1,2,3]{2,1,0:T(2,128)}, u32[]{:S(2)}) copy-start(s32[1,2,3]{2,1,0:T(2,128)} %param.8) | copy-start | bytes 76
  23.3 21.5 %collective-permute-start.1 = (bf16[128,3,896]{2,0,1:T(8,128)(2,1)S(1)}, bf16[128,3,896]{2,0,1:T(8,128)(2,1)}, u32[]{:S(2)}, u32[]{:S(2)}) collective-permute-start(bf16[128,3,896]{2,0,1:T(8,128)(2,1)S(1)} %fusion.25), channel_id=1, source_target_pairs={{0,8},{8,16},{16,24},{24,0},{1,9},{9,17},{17,25},{25,1},{2,10},{10... | collective-permute-start | bytes 2064392 | tf_op jit(solution)/shard_map/ppermute | solution.py:14
  45.2 1.4 %copy-start.1 = (bf16[128,3,896]{0,2,1:T(8,128)(2,1)}, bf16[128,3,896]{0,2,1:T(8,128)(2,1)S(1)}, u32[]{:S(2)}) copy-start(bf16[128,3,896]{0,2,1:T(8,128)(2,1)S(1)} %copy.47) | copy-start | bytes 2064388
  45.6 5.5 %copy-start.4 = (f32[8,128,128]{1,2,0:T(8,128)}, f32[8,128,128]{1,2,0:T(8,128)S(1)}, u32[]{:S(2)}) copy-start(f32[8,128,128]{1,2,0:T(8,128)S(1)} %get-tuple-element.31) | copy-start | bytes 1572868
  51.1 1.0 copy-start.8
  51.1 1.0 copy-start.9
  54.4 0.8 copy-start.3
  56.2 1.0 copy-start.7
  57.2 1.1 copy-start.6
  59.9 1.8 %slice-start = ((bf16[320,896]{1,0:T(8,128)(2,1)}), bf16[128,896]{1,0:T(8,128)(2,1)S(1)}, s32[]{:S(2)}) async-start(bf16[320,896]{1,0:T(8,128)(2,1)} %copy-done.3), calls=%async_computation.3 | async-start | bytes 458752 | tf_op jit(solution)/shard_map/slice | solution.py:111
  59.9 2.0 %copy-start.2 = (bf16[128,3,896]{0,2,1:T(8,128)(2,1)S(1)}, bf16[128,3,896]{0,2,1:T(8,128)(2,1)}, u32[]{:S(2)}) copy-start(bf16[128,3,896]{0,2,1:T(8,128)(2,1)} %copy-done.1) | copy-start | bytes 2064388
  59.9 2.0 %copy-start.5 = (f32[8,128,128]{1,2,0:T(8,128)S(1)}, f32[8,128,128]{1,2,0:T(8,128)}, u32[]{:S(2)}) copy-start(f32[8,128,128]{1,2,0:T(8,128)} %copy-done.4) | copy-start | bytes 1572868
Sparse Core Ops, SparseCore 0:
  10.7 28.5 all-gather.1
Sparse Core Ops, SparseCore 1:
  51.2 36.3 reduce-scatter.1
where the time goes:
time: 129 us; the launch traced here: 128 us
  blocking collectives  32.4 us (25%)
  waiting for transfers between devices  30.6 us (24%)
  between operations  20.9 us (16%)
  local copies, waits for them, and re-layouts  16.4 us (13%)
  matrix products  13.6 us (11%)
  other arithmetic  9.48 us (7%)
  starting transfers between devices  4.82 us (4%)
    psum x1, blocking collectives, local(): whole = lax.psum(rank_sum, 'fsdp')  32.4 us
    reduce_scatter x1, waiting for transfers between devices, local(): lax.psum_scatter(lax.dot_general(cot_all, mixed_all, (((0,), (0,)), ((),...  23.1 us
    ppermute x2, waiting for transfers between devices, passed_along(): lax.ppermute(shard, axis, [(i, (i + by) % length) for i in range(length)])  6.79 us
    unnamed x25, local copies, waits for them, and re-layouts  5.33 us
    ppermute x2, starting transfers between devices, passed_along(): lax.ppermute(shard, axis, [(i, (i + by) % length) for i in range(length)])  4.74 us
    dot_general x6, matrix products, attend(): jnp.einsum('hqk,khd->qhd', probs, values, preferred_element_type=jnp.floa...  3.77 us
    dot_general x1, matrix products, local(): lax.dot_general(cot_all, mixed_all, (((0,), (0,)), ((), ())), preferred_e...  3.45 us
    convert_element_type x3, local copies, waits for them, and re-layouts, attend(): return mixed.reshape(length, HEADS * HSIZE).astype(jnp.bfloat16)  3.38 us
  transfers between devices with their start and end apart: 4, of which 2 were waited for; matrix products, arithmetic and copies ran while one was open for 28% of the time, Pallas kernels for 0%

commit v1 on v0

--- a/solution.py
+++ b/solution.py
@@ -1,6 +1,8 @@
 import jax
 import jax.numpy as jnp
 from jax import lax
+from jax.experimental import pallas as pl
+from jax.experimental.pallas import tpu as pltpu
 from jax.sharding import PartitionSpec as P
 
 HEADS = 8
@@ -124,7 +126,239 @@
     return (grad_home[None, None], grad_box[None, None], weight_grad)
 
 
+F32 = jnp.float32
+BF16 = jnp.bfloat16
+CUT = 64
+
+
+def dot(a, b, dims):
+    return lax.dot_general(a, b, ((dims[:1], dims[1:]), ((), ())), preferred_element_type=F32)
+
+
+def block_kernel(
+    lens_ref, moves_ref, qkv_ref, g_ref, w_ref,
+    home_ref, box_ref, wg_ref,
+    w_all, probs, backs, t_own, t_core, chip, x_first, y_first, x_mid, y_mid, x_last, y_last,
+    z_out, z_in, box_out,
+    w_send, w_recv, c_send, c_recv, r_send, r_recv, z_send, z_recv, b_send, b_recv,
+):
+    rank, col = lax.axis_index("dp"), lax.axis_index("fsdp")
+    core = lax.rem(col, 2)
+    px = lax.rem(col // 2, 2)
+    py = col // 4
+    other_core = col + 1 - 2 * core
+    other_x = col + 2 - 4 * px
+    other_y = col + 4 - 8 * py
+    diagonal = other_x + 4 - 8 * py
+    n_dp = lax.axis_size("dp")
+    pad = HSIZE
+
+    def to_col(target):
+        return {"dp": rank, "fsdp": target}
+
+    def to_rank(target):
+        return {"dp": target, "fsdp": col}
+
+    def push(src, dst, send, recv, target):
+        copy = pltpu.make_async_remote_copy(
+            src_ref=src, dst_ref=dst, send_sem=send, recv_sem=recv,
+            device_id=target, device_id_type=pl.DeviceIdType.MESH,
+        )
+        copy.start()
+        return copy
+
+    barrier = pltpu.get_barrier_semaphore()
+    partners = [to_col(other_core), to_col(other_x), to_col(other_y)]
+    partners += [to_rank(lax.rem(rank + k, n_dp)) for k in range(1, n_dp)]
+    for partner in partners:
+        pl.semaphore_signal(barrier, inc=1, device_id=partner, device_id_type=pl.DeviceIdType.MESH)
+    pl.semaphore_wait(barrier, len(partners))
+
+    def w_rows(owner, begin=0, count=pad):
+        return w_all.at[pl.ds(pl.multiple_of(owner * pad + begin, 16), count)]
+
+    def w_push(slot, src, owner, target, begin=0, count=pad):
+        return push(src, w_rows(owner, begin, count), w_send.at[slot], w_recv.at[slot], to_col(target))
+
+    started = []
+    w_x = w_push(0, w_ref, col, other_x)
+    w_y = w_push(1, w_ref, col, other_y)
+    w_c = w_push(2, w_ref, col, other_core)
+    started += [w_x, w_y, w_c]
+    w_all[pl.ds(pl.multiple_of(col * pad, 16), pad)] = w_ref[...]
+
+    l0, l1, l2 = lens_ref[rank, 0], lens_ref[rank, 1], lens_ref[rank, 2]
+    e0, e1 = l0, l0 + l1
+    n_tok = g_ref.shape[0]
+
+    def seg_of(places):
+        return (places >= e0).astype(jnp.int32) + (places >= e1).astype(jnp.int32)
+
+    allowed = seg_of(lax.broadcasted_iota(jnp.int32, (n_tok, n_tok), 0)) == seg_of(
+        lax.broadcasted_iota(jnp.int32, (n_tok, n_tok), 1))
+    gone = []
+    for clip in range(3):
+        flag = jnp.int32(0)
+        for m in range(moves_ref.shape[0]):
+            hit = jnp.logical_and(moves_ref[m, 0] == rank, moves_ref[m, 2] == clip)
+            flag = jnp.where(hit, jnp.int32(1), flag)
+        gone.append(flag)
+    start, count = jnp.int32(0), jnp.int32(0)
+    for m in range(moves_ref.shape[0]):
+        mine, which = moves_ref[m, 0] == rank, moves_ref[m, 2]
+        begin = jnp.where(which == 0, jnp.int32(0), jnp.where(which == 1, e0, e1))
+        length = jnp.where(which == 0, l0, jnp.where(which == 1, l1, l2))
+        start = jnp.where(mine, begin, start)
+        count = jnp.where(mine, length, count)
+    seg_row = seg_of(lax.broadcasted_iota(jnp.int32, (1, n_tok), 1))
+    gone_row = jnp.where(seg_row == 0, gone[0], jnp.where(seg_row == 1, gone[1], gone[2]))
+    stay_row = (1 - gone_row).astype(F32)
+    pick_t = lax.broadcasted_iota(jnp.int32, (n_tok, CLIP_MAX), 0)
+    pick_i = lax.broadcasted_iota(jnp.int32, (n_tok, CLIP_MAX), 1)
+    picked = jnp.logical_and(pick_t == pick_i + start, pick_i < count)
+    pick = jnp.where(picked, jnp.float32(1), jnp.float32(0)).astype(BF16)
+
+    cot = g_ref[...]
+    c_copies = []
+    for h in range(HEADS):
+        rows = pl.ds(h * pad, pad)
+        q, k, v = qkv_ref[0, rows], qkv_ref[1, rows], qkv_ref[2, rows]
+        scores = dot(k, q, (0, 0)) * HSIZE ** (-0.5)
+        scores = jnp.where(allowed, scores, -1000000000.0)
+        top = jnp.max(scores, axis=0, keepdims=True)
+        e = jnp.exp(scores - top)
+        p = (e * (1.0 / jnp.sum(e, axis=0, keepdims=True))).astype(BF16)
+        probs[h] = p
+        mixed = dot(v, p, (1, 0)).astype(BF16)
+        t_own[h % 2, h // 2] = dot(mixed, cot, (1, 0)).astype(BF16)
+        if h % 2 == 1:
+            m = h // 2
+            c_copies.append(push(t_own.at[1 - core, m], t_core.at[m], c_send.at[m], c_recv.at[m], to_col(other_core)))
+        if h == 3:
+            w_x.wait_recv()
+            diag_a = w_push(3, w_rows(other_x, 0, CUT), other_x, other_y, 0, CUT)
+            pass_x = w_push(5, w_rows(other_x), other_x, other_core)
+            w_y.wait_recv()
+            diag_b = w_push(4, w_rows(other_y, CUT, pad - CUT), other_y, other_x, CUT, pad - CUT)
+            pass_y = w_push(6, w_rows(other_y), other_y, other_core)
+            started += [diag_a, pass_x, diag_b, pass_y]
+    started += c_copies
+
+    def r_push(slot, src, dst, target):
+        copy = push(src, dst, r_send.at[slot], r_recv.at[slot], to_col(target))
+        started.append(copy)
+        return copy
+
+    low, high = pl.ds(0, CUT), pl.ds(CUT, pad - CUT)
+    for m in range(4):
+        c_copies[m].wait_recv()
+        chip[m] = (t_own[core, m].astype(F32) + t_core[m].astype(F32)).astype(BF16)
+    to_x = [r_push(i, chip.at[2 * i + 1 - px, low], x_first.at[i], other_x) for i in range(2)]
+    to_y = [r_push(2 + i, chip.at[2 * (1 - py) + i, high], y_first.at[i], other_y) for i in range(2)]
+
+    diag_a.wait_recv()
+    pass_a = w_push(7, w_rows(diagonal, 0, CUT), diagonal, other_core, 0, CUT)
+    diag_b.wait_recv()
+    pass_b = w_push(8, w_rows(diagonal, CUT, pad - CUT), diagonal, other_core, CUT, pad - CUT)
+    started += [pass_a, pass_b]
+    for copy in (w_c, pass_x, pass_y, pass_a, pass_b):
+        copy.wait_recv()
+    backs[...] = dot(w_all[...], cot, (1, 1)).astype(BF16)
+
+    boxes = []
+    for h in range(HEADS):
+        rows = pl.ds(h * pad, pad)
+        q, k, v = qkv_ref[0, rows], qkv_ref[1, rows], qkv_ref[2, rows]
+        p, back = probs[h], backs[rows]
+        dp = dot(v, back, (0, 0))
+        pf = p.astype(F32)
+        ds = pf * (dp - jnp.sum(pf * dp, axis=0, keepdims=True))
+        ds = (ds * HSIZE ** (-0.5)).astype(BF16)
+        grads = (dot(k, ds, (1, 0)), dot(q, ds, (1, 1)), dot(back, p, (1, 1)))
+        for i, grad in enumerate(grads):
+            home_ref[i, rows] = (grad * stay_row).astype(BF16)
+            box_out[h, i] = dot(grad.astype(BF16), pick, (1, 0)).astype(BF16)
+        boxes.append(push(box_out.at[h], box_ref.at[h], b_send.at[h], b_recv.at[h], to_rank(lax.rem(rank + 1, n_dp))))
+        if h == 2:
+            for i in range(2):
+                to_x[i].wait_recv()
+                x_mid[i] = (chip[2 * i + px, low].astype(F32) + x_first[i].astype(F32)).astype(BF16)
+                to_y[i].wait_recv()
+                y_mid[i] = (chip[2 * py + i, high].astype(F32) + y_first[i].astype(F32)).astype(BF16)
+            then_y = r_push(4, x_mid.at[1 - py], y_last, other_y)
+            then_x = r_push(5, y_mid.at[1 - px], x_last, other_x)
+        if h == 5:
+            then_y.wait_recv()
+            then_x.wait_recv()
+            own_low = x_mid[py].astype(F32) + y_last[...].astype(F32)
+            own_high = y_mid[px].astype(F32) + x_last[...].astype(F32)
+            width = z_out.shape[2]
+            for part in range(n_dp):
+                cut = slice(part * width, (part + 1) * width)
+                z_out[part, low] = own_low[:, cut].astype(BF16)
+                z_out[part, high] = own_high[:, cut].astype(BF16)
+            z_copies = []
+            for step in range(1, n_dp):
+                target = lax.rem(rank + step, n_dp)
+                z_copies.append(push(z_out.at[target], z_in.at[step - 1], z_send.at[step - 1], z_recv.at[step - 1], to_rank(target)))
+    started += boxes + z_copies
+    total = z_out[rank].astype(F32)
+    for step, copy in enumerate(z_copies):
+        copy.wait_recv()
+        total += z_in[step].astype(F32)
+    wg_ref[...] = total
+    for copy in boxes:
+        copy.wait_recv()
+    for copy in started:
+        copy.wait_send()
+
+
+def fused(qkv, grad_out, lengths, moves, out_weight):
+    n_dp = lax.axis_size("dp")
+    tok, feats = qkv.shape[2], qkv.shape[4]
+    dout = grad_out.shape[3]
+    pad, rest, width = HSIZE, HSIZE - CUT, dout // n_dp
+    vmem = pl.BlockSpec(memory_space=pltpu.VMEM)
+    smem = pl.BlockSpec(memory_space=pltpu.SMEM)
+    features = jnp.transpose(qkv[0, 0], (1, 2, 0))
+    home, box, weight_grad = pl.pallas_call(
+        block_kernel,
+        out_shape=(
+            jax.ShapeDtypeStruct((3, feats, tok), BF16),
+            jax.ShapeDtypeStruct((HEADS, 3, pad, CLIP_MAX), BF16),
+            jax.ShapeDtypeStruct((pad, width), F32),
+        ),
+        in_specs=[smem, smem, vmem, vmem, vmem],
+        out_specs=(vmem, vmem, vmem),
+        scratch_shapes=[
+            pltpu.VMEM((feats, dout), BF16),
+            pltpu.VMEM((HEADS, tok, tok), BF16),
+            pltpu.VMEM((feats, tok), BF16),
+            pltpu.VMEM((2, 4, pad, dout), BF16),
+            pltpu.VMEM((4, pad, dout), BF16),
+            pltpu.VMEM((4, pad, dout), BF16),
+            pltpu.VMEM((2, CUT, dout), BF16),
+            pltpu.VMEM((2, rest, dout), BF16),
+            pltpu.VMEM((2, CUT, dout), BF16),
+            pltpu.VMEM((2, rest, dout), BF16),
+            pltpu.VMEM((rest, dout), BF16),
+            pltpu.VMEM((CUT, dout), BF16),
+            pltpu.VMEM((n_dp, pad, width), BF16),
+            pltpu.VMEM((n_dp - 1, pad, width), BF16),
+            pltpu.VMEM((HEADS, 3, pad, CLIP_MAX), BF16),
+        ] + [pltpu.SemaphoreType.DMA((n,)) for n in (9, 9, 4, 4, 6, 6, n_dp - 1, n_dp - 1, HEADS, HEADS)],
+        compiler_params=pltpu.CompilerParams(
+            collective_id=0, has_side_effects=True, vmem_limit_bytes=40 * 1024 * 1024
+        ),
+        name="block",
+    )(lengths[:, 0], moves[0], features, grad_out[0, 0], out_weight)
+    home_grad = jnp.transpose(home, (2, 0, 1))
+    inbox_grad = jnp.transpose(box, (3, 1, 0, 2)).reshape(CLIP_MAX, 3, feats)
+    return (home_grad[None, None], inbox_grad[None, None], weight_grad)
+
+
 def solution(mesh):
+    small = mesh.shape["dp"] == 4 and mesh.shape["fsdp"] == 8
     placed = (
         P("dp", "fsdp", None, None, None),
         P("dp", "fsdp", None, None),
@@ -133,7 +367,7 @@
         P("fsdp", None),
     )
     return jax.shard_map(
-        local,
+        fused if small else local,
         mesh=mesh,
         in_specs=placed,
         out_specs=(

time: 129 us -> 50.9 us (0.39)
  Pallas kernels: 0 us -> 40.1 us
  blocking collectives: 32.4 us -> 0 us
  waiting for transfers between devices: 30.6 us -> 0 us
  between operations: 20.9 us -> 0.66 us
  matrix products: 13.6 us -> 0 us
  other arithmetic: 9.48 us -> 0 us
  local copies, waits for them, and re-layouts: 16.4 us -> 9.84 us
  starting transfers between devices: 4.82 us -> 0 us
    pallas_call x0 -> x1, Pallas kernels: none -> 40.1 us  [fused(): pl.pallas_call(block_kernel, out_shape=(jax.ShapeDtypeStruct((3, feats, t...]
    psum x1 -> x0, blocking collectives: 32.4 us -> none  [local(): whole = lax.psum(rank_sum, 'fsdp')]
    reduce_scatter x1 -> x0, waiting for transfers between devices: 23.1 us -> none  [local(): lax.psum_scatter(lax.dot_general(cot_all, mixed_all, (((0,), (0,)), ((),...]
    dot_general x12 -> x0, matrix products: 11.4 us -> none  [the longest x6 3.77 us: attend(): jnp.einsum('hqk,khd->qhd', probs, values, preferred_element_type=jnp.floa...]
    ppermute x2 -> x0, waiting for transfers between devices: 6.79 us -> none  [passed_along(): lax.ppermute(shard, axis, [(i, (i + by) % length) for i in range(length)])]
    ppermute x2 -> x0, starting transfers between devices: 4.74 us -> none  [passed_along(): lax.ppermute(shard, axis, [(i, (i + by) % length) for i in range(length)])]
    unnamed x25 -> x13, local copies, waits for them, and re-layouts: 5.33 us -> 9.8 us
    select_n x4 -> x0, other arithmetic: 3.72 us -> none  [the longest x1 1.69 us: local(): jnp.where(sending, lax.dynamic_slice_in_dim(cot_pad, send_off, CLIP_MAX,...]
  transfers between devices with their start and end apart: 4 -> 0, of which waited for: 2 -> 0; matrix products, arithmetic and copies ran while one was open for 28% -> 0% of each run, Pallas kernels for 0% -> 0%
where the time goes in v1:
time: 50.9 us; the launch traced here: 50.6 us
  Pallas kernels  40.1 us (79%)
  local copies, waits for them, and re-layouts  9.84 us (19%)
  between operations  0.66 us (1%)
    pallas_call x1, Pallas kernels, fused(): pl.pallas_call(block_kernel, out_shape=(jax.ShapeDtypeStruct((3, feats, t...  40.1 us
    unnamed x13, local copies, waits for them, and re-layouts  9.8 us

profile of v1, /device:TPU:0, one launch (start us, length us, event | category | flops | bytes accessed | tf_op | source)
XLA Modules:
  0.0 50.6 jit_solution(8143212751136486824)
XLA Ops:
  0.6 1.3 %copy.11 = s32[4,1,3]{2,0,1:T(4,128)} copy(s32[4,1,3]{0,1,2:T(1,128)} %param.7) | data formatting | bytes 96 | tf_op args[2]
  2.0 1.9 %copy.12 = bf16[1,1,192,3,896]{2,4,3,1,0:T(8,128)(2,1)S(1)} copy(bf16[1,1,192,3,896]{4,2,3,1,0:T(8,128)(2,1)} %param.5) | data formatting | bytes 2064384 | tf_op args[0]
  3.8 0.0 copy-start
  3.8 1.0 %copy-done = bf16[1,1,192,896]{3,2,1,0:T(8,128)(2,1)S(1)} copy-done((bf16[1,1,192,896]{3,2,1,0:T(8,128)(2,1)S(1)}, bf16[1,1,192,896]{3,2,1,0:T(8,128)(2,1)}, u32[]{:S(2)}) %copy-start) | copy-done | bytes 344088
  4.8 0.0 copy-start.1
  4.8 0.9 %copy-done.1 = bf16[112,896]{1,0:T(8,128)(2,1)S(1)} copy-done((bf16[112,896]{1,0:T(8,128)(2,1)S(1)}, bf16[112,896]{1,0:T(8,128)(2,1)}, u32[]{:S(2)}) %copy-start.1) | copy-done | bytes 200728
  5.7 0.0 copy-start.2
  5.7 0.7 %copy-done.2 = s32[4,1,3]{2,0,1:T(4,128)S(1)} copy-done((s32[4,1,3]{2,0,1:T(4,128)S(1)}, s32[4,1,3]{2,0,1:T(4,128)}, u32[]{:S(2)}) %copy-start.2) | copy-done | bytes 72
  6.4 0.0 copy-start.3
  6.4 0.7 %copy-done.3 = s32[1,2,3]{2,1,0:T(2,128)S(1)} copy-done((s32[1,2,3]{2,1,0:T(2,128)S(1)}, s32[1,2,3]{2,1,0:T(2,128)}, u32[]{:S(2)}) %copy-start.3) | copy-done | bytes 48
  7.1 40.1 %block.1 = (bf16[3,896,192]{2,1,0:T(8,128)(2,1)S(1)}, bf16[8,3,112,128]{3,2,1,0:T(8,128)(2,1)S(1)}, f32[112,224]{1,0:T(8,128)S(1)}) custom-call(s32[4,3]{1,0:T(4,128)S(1)} %bitcast.15, s32[2,3]{1,0:T(2,128)S(1)} %bitcast.16, bf16[3,896,192]{2,1,0:T(8,128)(2,1)S(1)} %bitcast.11, bf16[192,896]{1,0:T(8,128)(2,1)S(1)} %bitcast.14, bf16[112,896]{1,0:T(8,128)(2,1)S(1)} %copy-done.1), custom_call_target="tpu_custom_call" | custom-call | tf_op jit(solution)/shard_map/block/pallas_call | solution.py:324
  47.2 1.6 %copy.14 = bf16[1,1,192,3,896]{4,2,3,1,0:T(8,128)(2,1)} copy(bf16[1,1,192,3,896]{2,4,3,1,0:T(8,128)(2,1)S(1)} %bitcast.12) | data formatting | bytes 2064384
  48.8 1.1 %copy.15 = bf16[1,1,128,3,896]{4,2,3,1,0:T(8,128)(2,1)} copy(bf16[1,1,128,3,896]{2,4,3,1,0:T(8,128)(2,1)S(1)} %bitcast.17) | data formatting | bytes 1376256
  49.9 0.6 %copy.17 = f32[112,224]{1,0:T(8,128)} copy(f32[112,224]{1,0:T(8,128)S(1)} %get-tuple-element.20) | data formatting | bytes 200704
  (1 shorter events, 0.0 us)
Async XLA Ops:
  3.8 1.0 %copy-start = (bf16[1,1,192,896]{3,2,1,0:T(8,128)(2,1)S(1)}, bf16[1,1,192,896]{3,2,1,0:T(8,128)(2,1)}, u32[]{:S(2)}) copy-start(bf16[1,1,192,896]{3,2,1,0:T(8,128)(2,1)} %param.6) | copy-start | bytes 1032196
  4.8 0.9 %copy-start.1 = (bf16[112,896]{1,0:T(8,128)(2,1)S(1)}, bf16[112,896]{1,0:T(8,128)(2,1)}, u32[]{:S(2)}) copy-start(bf16[112,896]{1,0:T(8,128)(2,1)} %w_ref.1) | copy-start | bytes 602116
  5.7 0.7 %copy-start.2 = (s32[4,1,3]{2,0,1:T(4,128)S(1)}, s32[4,1,3]{2,0,1:T(4,128)}, u32[]{:S(2)}) copy-start(s32[4,1,3]{2,0,1:T(4,128)} %copy.11) | copy-start | bytes 148
  6.4 0.7 %copy-start.3 = (s32[1,2,3]{2,1,0:T(2,128)S(1)}, s32[1,2,3]{2,1,0:T(2,128)}, u32[]{:S(2)}) copy-start(s32[1,2,3]{2,1,0:T(2,128)} %param.8) | copy-start | bytes 76

commit v2 on v1

--- a/solution.py
+++ b/solution.py
@@ -136,11 +136,11 @@
 
 
 def block_kernel(
-    lens_ref, moves_ref, qkv_ref, g_ref, w_ref,
+    lens_hbm, moves_hbm, qkv_hbm, g_hbm, w_ref,
     home_ref, box_ref, wg_ref,
-    w_all, probs, backs, t_own, t_core, chip, x_first, y_first, x_mid, y_mid, x_last, y_last,
+    lens_ref, moves_ref, nat_ref, qkv_ref, g_ref, home_t, box_in, w_all, probs, backs, t_own, t_core, chip, x_first, y_first, x_mid, y_mid, x_last, y_last,
     z_out, z_in, box_out,
-    w_send, w_recv, c_send, c_recv, r_send, r_recv, z_send, z_recv, b_send, b_recv,
+    in_sem, w_send, w_recv, c_send, c_recv, r_send, r_recv, z_send, z_recv, b_send, b_recv,
 ):
     rank, col = lax.axis_index("dp"), lax.axis_index("fsdp")
     core = lax.rem(col, 2)
@@ -167,6 +167,14 @@
         copy.start()
         return copy
 
+    fetches = [
+        pltpu.make_async_copy(src, dst, in_sem.at[i]) for i, (src, dst) in enumerate((
+            (lens_hbm, lens_ref), (moves_hbm, moves_ref), (qkv_hbm.at[0], nat_ref.at[0]),
+            (qkv_hbm.at[1], nat_ref.at[1]), (qkv_hbm.at[2], nat_ref.at[2]), (g_hbm, g_ref),
+            (w_ref, w_all.at[pl.ds(pl.multiple_of(col * pad, 16), pad)])))
+    ]
+    for fetch in fetches:
+        fetch.start()
     barrier = pltpu.get_barrier_semaphore()
     partners = [to_col(other_core), to_col(other_x), to_col(other_y)]
     partners += [to_rank(lax.rem(rank + k, n_dp)) for k in range(1, n_dp)]
@@ -185,9 +193,12 @@
     w_y = w_push(1, w_ref, col, other_y)
     w_c = w_push(2, w_ref, col, other_core)
     started += [w_x, w_y, w_c]
-    w_all[pl.ds(pl.multiple_of(col * pad, 16), pad)] = w_ref[...]
-
-    l0, l1, l2 = lens_ref[rank, 0], lens_ref[rank, 1], lens_ref[rank, 2]
+    for fetch in fetches:
+        fetch.wait()
+    for i in range(3):
+        qkv_ref[i] = nat_ref[i].T
+
+    l0, l1, l2 = lens_ref[0, 0, rank], lens_ref[1, 0, rank], lens_ref[2, 0, rank]
     e0, e1 = l0, l0 + l1
     n_tok = g_ref.shape[0]
 
@@ -199,13 +210,13 @@
     gone = []
     for clip in range(3):
         flag = jnp.int32(0)
-        for m in range(moves_ref.shape[0]):
-            hit = jnp.logical_and(moves_ref[m, 0] == rank, moves_ref[m, 2] == clip)
+        for m in range(moves_ref.shape[1]):
+            hit = jnp.logical_and(moves_ref[0, m, 0] == rank, moves_ref[0, m, 2] == clip)
             flag = jnp.where(hit, jnp.int32(1), flag)
         gone.append(flag)
     start, count = jnp.int32(0), jnp.int32(0)
-    for m in range(moves_ref.shape[0]):
-        mine, which = moves_ref[m, 0] == rank, moves_ref[m, 2]
+    for m in range(moves_ref.shape[1]):
+        mine, which = moves_ref[0, m, 0] == rank, moves_ref[0, m, 2]
         begin = jnp.where(which == 0, jnp.int32(0), jnp.where(which == 1, e0, e1))
         length = jnp.where(which == 0, l0, jnp.where(which == 1, l1, l2))
         start = jnp.where(mine, begin, start)
@@ -222,8 +233,8 @@
     c_copies = []
     for h in range(HEADS):
         rows = pl.ds(h * pad, pad)
-        q, k, v = qkv_ref[0, rows], qkv_ref[1, rows], qkv_ref[2, rows]
-        scores = dot(k, q, (0, 0)) * HSIZE ** (-0.5)
+        q, k, v = qkv_ref[0, rows], nat_ref[1, :, h * pad:(h + 1) * pad], qkv_ref[2, rows]
+        scores = dot(k, q, (1, 0)) * HSIZE ** (-0.5)
         scores = jnp.where(allowed, scores, -1000000000.0)
         top = jnp.max(scores, axis=0, keepdims=True)
         e = jnp.exp(scores - top)
@@ -268,17 +279,17 @@
     boxes = []
     for h in range(HEADS):
         rows = pl.ds(h * pad, pad)
-        q, k, v = qkv_ref[0, rows], qkv_ref[1, rows], qkv_ref[2, rows]
+        q, k, v = qkv_ref[0, rows], qkv_ref[1, rows], nat_ref[2, :, h * pad:(h + 1) * pad]
         p, back = probs[h], backs[rows]
-        dp = dot(v, back, (0, 0))
+        dp = dot(v, back, (1, 0))
         pf = p.astype(F32)
         ds = pf * (dp - jnp.sum(pf * dp, axis=0, keepdims=True))
         ds = (ds * HSIZE ** (-0.5)).astype(BF16)
         grads = (dot(k, ds, (1, 0)), dot(q, ds, (1, 1)), dot(back, p, (1, 1)))
         for i, grad in enumerate(grads):
-            home_ref[i, rows] = (grad * stay_row).astype(BF16)
-            box_out[h, i] = dot(grad.astype(BF16), pick, (1, 0)).astype(BF16)
-        boxes.append(push(box_out.at[h], box_ref.at[h], b_send.at[h], b_recv.at[h], to_rank(lax.rem(rank + 1, n_dp))))
+            home_t[i, rows] = (grad * stay_row).astype(BF16)
+            box_out[i, h] = dot(grad.astype(BF16), pick, (1, 0)).astype(BF16)
+        boxes.append(push(box_out.at[:, h], box_in.at[:, h], b_send.at[h], b_recv.at[h], to_rank(lax.rem(rank + 1, n_dp))))
         if h == 2:
             for i in range(2):
                 to_x[i].wait_recv()
@@ -302,6 +313,8 @@
                 target = lax.rem(rank + step, n_dp)
                 z_copies.append(push(z_out.at[target], z_in.at[step - 1], z_send.at[step - 1], z_recv.at[step - 1], to_rank(target)))
     started += boxes + z_copies
+    for i in range(3):
+        home_ref[i] = home_t[i].T
     total = z_out[rank].astype(F32)
     for step, copy in enumerate(z_copies):
         copy.wait_recv()
@@ -309,6 +322,8 @@
     wg_ref[...] = total
     for copy in boxes:
         copy.wait_recv()
+    for i in range(3):
+        box_ref[i] = box_in[i].reshape(HEADS * pad, CLIP_MAX).T
     for copy in started:
         copy.wait_send()
 
@@ -319,18 +334,26 @@
     dout = grad_out.shape[3]
     pad, rest, width = HSIZE, HSIZE - CUT, dout // n_dp
     vmem = pl.BlockSpec(memory_space=pltpu.VMEM)
-    smem = pl.BlockSpec(memory_space=pltpu.SMEM)
-    features = jnp.transpose(qkv[0, 0], (1, 2, 0))
+    hbm = pl.BlockSpec(memory_space=pltpu.HBM)
+    natural = jnp.transpose(qkv[0, 0], (1, 0, 2))
+    by_clip = jnp.transpose(lengths, (2, 1, 0))
     home, box, weight_grad = pl.pallas_call(
         block_kernel,
         out_shape=(
-            jax.ShapeDtypeStruct((3, feats, tok), BF16),
-            jax.ShapeDtypeStruct((HEADS, 3, pad, CLIP_MAX), BF16),
+            jax.ShapeDtypeStruct((3, tok, feats), BF16),
+            jax.ShapeDtypeStruct((3, CLIP_MAX, feats), BF16),
             jax.ShapeDtypeStruct((pad, width), F32),
         ),
-        in_specs=[smem, smem, vmem, vmem, vmem],
+        in_specs=[hbm] * 5,
         out_specs=(vmem, vmem, vmem),
         scratch_shapes=[
+            pltpu.SMEM(by_clip.shape, jnp.int32),
+            pltpu.SMEM(moves.shape, jnp.int32),
+            pltpu.VMEM((3, tok, feats), BF16),
+            pltpu.VMEM((3, feats, tok), BF16),
+            pltpu.VMEM((tok, dout), BF16),
+            pltpu.VMEM((3, feats, tok), BF16),
+            pltpu.VMEM((3, HEADS, pad, CLIP_MAX), BF16),
             pltpu.VMEM((feats, dout), BF16),
             pltpu.VMEM((HEADS, tok, tok), BF16),
             pltpu.VMEM((feats, tok), BF16),
@@ -345,15 +368,15 @@
             pltpu.VMEM((CUT, dout), BF16),
             pltpu.VMEM((n_dp, pad, width), BF16),
             pltpu.VMEM((n_dp - 1, pad, width), BF16),
-            pltpu.VMEM((HEADS, 3, pad, CLIP_MAX), BF16),
-        ] + [pltpu.SemaphoreType.DMA((n,)) for n in (9, 9, 4, 4, 6, 6, n_dp - 1, n_dp - 1, HEADS, HEADS)],
+            pltpu.VMEM((3, HEADS, pad, CLIP_MAX), BF16),
+        ] + [pltpu.SemaphoreType.DMA((n,)) for n in (7, 9, 9, 4, 4, 6, 6, n_dp - 1, n_dp - 1, HEADS, HEADS)],
         compiler_params=pltpu.CompilerParams(
-            collective_id=0, has_side_effects=True, vmem_limit_bytes=40 * 1024 * 1024
+            collective_id=0, has_side_effects=True, vmem_limit_bytes=60 * 1024 * 1024
         ),
         name="block",
-    )(lengths[:, 0], moves[0], features, grad_out[0, 0], out_weight)
-    home_grad = jnp.transpose(home, (2, 0, 1))
-    inbox_grad = jnp.transpose(box, (3, 1, 0, 2)).reshape(CLIP_MAX, 3, feats)
+    )(by_clip, moves, natural, grad_out[0, 0], out_weight)
+    home_grad = jnp.transpose(home, (1, 0, 2))
+    inbox_grad = jnp.transpose(box, (1, 0, 2))
     return (home_grad[None, None], inbox_grad[None, None], weight_grad)
 
 

time: 50.9 us -> 46.1 us (0.906)
  local copies, waits for them, and re-layouts: 9.84 us -> 3.97 us
  Pallas kernels: 40.1 us -> 41.3 us
    unnamed x13 -> x7, local copies, waits for them, and re-layouts: 9.8 us -> 3.97 us
    pallas_call x1, Pallas kernels: 40.1 us -> 41.3 us  [fused(): pl.pallas_call(block_kernel, out_shape=(jax.ShapeDtypeStruct((3, tok, fea...]
where the time goes in v2:
time: 46.1 us; the launch traced here: 45.9 us
  Pallas kernels  41.3 us (90%)
  local copies, waits for them, and re-layouts  3.97 us (9%)
  between operations  0.65 us (1%)
    pallas_call x1, Pallas kernels, fused(): pl.pallas_call(block_kernel, out_shape=(jax.ShapeDtypeStruct((3, tok, fea...  41.3 us
    unnamed x7, local copies, waits for them, and re-layouts  3.97 us

profile of v2, /device:TPU:0, one launch (start us, length us, event | category | flops | bytes accessed | tf_op | source)
XLA Modules:
  0.0 45.9 jit_solution(12388378483194559662)
XLA Ops:
  0.6 41.3 %block.1 = (bf16[3,192,896]{2,1,0:T(8,128)(2,1)}, bf16[3,128,896]{2,1,0:T(8,128)(2,1)}, f32[112,224]{1,0:T(8,128)}) custom-call(s32[3,1,4]{2,1,0:T(1,128)} %bitcast.15, s32[1,2,3]{2,1,0:T(2,128)} %moves_hbm.1, bf16[3,192,896]{2,1,0:T(8,128)(2,1)} %bitcast.11, bf16[192,896]{1,0:T(8,128)(2,1)} %bitcast.14, bf16[112,896]{1,0:T(8,128)(2,1)} %w_ref.1), custom_call_target="tpu_custom_call" | custom-call | tf_op jit(solution)/shard_map/block/pallas_call | solution.py:340
  41.9 0.0 copy-start
  41.9 2.3 %copy.11 = bf16[1,1,192,3,896]{4,2,3,1,0:T(8,128)(2,1)} copy(bf16[1,1,192,3,896]{4,2,3,1,0:T(8,128)(2,1)} %bitcast.12) | data formatting | bytes 2064384
  44.3 0.0 copy-done
  44.3 0.0 copy-start.1
  44.3 0.8 %copy.12 = bf16[1,1,128,3,896]{4,2,3,1,0:T(8,128)(2,1)} copy(bf16[1,1,128,3,896]{4,2,3,1,0:T(8,128)(2,1)S(1)} %bitcast.13) | data formatting | bytes 1376256
  45.1 0.1 copy-done.1
  45.3 0.6 %copy.13 = f32[112,224]{1,0:T(8,128)} copy(f32[112,224]{1,0:T(8,128)S(1)} %copy-done.1) | data formatting | bytes 200704
Async XLA Ops:
  41.9 2.3 %copy-start = (bf16[3,128,896]{2,1,0:T(8,128)(2,1)S(1)}, bf16[3,128,896]{2,1,0:T(8,128)(2,1)}, u32[]{:S(2)}) copy-start(bf16[3,128,896]{2,1,0:T(8,128)(2,1)} %get-tuple-element.7) | copy-start | bytes 2064388
  44.3 1.0 %copy-start.1 = (f32[112,224]{1,0:T(8,128)S(1)}, f32[112,224]{1,0:T(8,128)}, u32[]{:S(2)}) copy-start(f32[112,224]{1,0:T(8,128)} %get-tuple-element.14) | copy-start | bytes 301060

commit v3 on v2

--- a/solution.py
+++ b/solution.py
@@ -128,6 +128,7 @@
 
 F32 = jnp.float32
 BF16 = jnp.bfloat16
+EARLY = 5
 CUT = 64
 
 
@@ -138,9 +139,9 @@
 def block_kernel(
     lens_hbm, moves_hbm, qkv_hbm, g_hbm, w_ref,
     home_ref, box_ref, wg_ref,
-    lens_ref, moves_ref, nat_ref, qkv_ref, g_ref, home_t, box_in, w_all, probs, backs, t_own, t_core, chip, x_first, y_first, x_mid, y_mid, x_last, y_last,
+    lens_ref, moves_ref, nat_ref, qkv_ref, g_ref, home_t, box_in, early_out, early_in, back_out, back_in, box_probs, w_all, probs, backs, t_own, t_core, chip, x_first, y_first, x_mid, y_mid, x_last, y_last,
     z_out, z_in, box_out,
-    in_sem, w_send, w_recv, c_send, c_recv, r_send, r_recv, z_send, z_recv, b_send, b_recv,
+    in_sem, w_send, w_recv, c_send, c_recv, r_send, r_recv, z_send, z_recv, b_send, b_recv, e_send, e_recv,
 ):
     rank, col = lax.axis_index("dp"), lax.axis_index("fsdp")
     core = lax.rem(col, 2)
@@ -229,16 +230,43 @@
     picked = jnp.logical_and(pick_t == pick_i + start, pick_i < count)
     pick = jnp.where(picked, jnp.float32(1), jnp.float32(0)).astype(BF16)
 
+    ahead = EARLY * pad
+    succ = to_rank(lax.rem(rank + 1, n_dp))
+
+    def e_push(slot, src, dst):
+        copy = push(src, dst, e_send.at[slot], e_recv.at[slot], succ)
+        started.append(copy)
+        return copy
+
+    early = []
+    for i in range(3):
+        early_out[i] = dot(qkv_ref[i, :ahead], pick, (1, 0)).astype(BF16)
+        early.append(e_push(i, early_out.at[i], early_in.at[i]))
+
+    pred = lax.rem(rank + n_dp - 1, n_dp)
+    arriving = jnp.int32(0)
+    for m in range(moves_ref.shape[1]):
+        which = moves_ref[0, m, 2]
+        length = jnp.where(which == 0, lens_ref[0, 0, pred], jnp.where(which == 1, lens_ref[1, 0, pred], lens_ref[2, 0, pred]))
+        arriving = jnp.where(moves_ref[0, m, 1] == rank, length, arriving)
+    box_allowed = lax.broadcasted_iota(jnp.int32, (CLIP_MAX, CLIP_MAX), 0) < arriving
+
+    def softmax(scores, mask):
+        scores = jnp.where(mask, scores, -1000000000.0)
+        e = jnp.exp((scores - jnp.max(scores, axis=0, keepdims=True)) * HSIZE ** (-0.5))
+        return (e * (1.0 / jnp.sum(e, axis=0, keepdims=True))).astype(BF16)
+
+    def score_grad(p, dp):
+        pf = p.astype(F32)
+        ds = pf * (dp - jnp.sum(pf * dp, axis=0, keepdims=True))
+        return (ds * HSIZE ** (-0.5)).astype(BF16)
+
     cot = g_ref[...]
     c_copies = []
     for h in range(HEADS):
         rows = pl.ds(h * pad, pad)
         q, k, v = qkv_ref[0, rows], nat_ref[1, :, h * pad:(h + 1) * pad], qkv_ref[2, rows]
-        scores = dot(k, q, (1, 0)) * HSIZE ** (-0.5)
-        scores = jnp.where(allowed, scores, -1000000000.0)
-        top = jnp.max(scores, axis=0, keepdims=True)
-        e = jnp.exp(scores - top)
-        p = (e * (1.0 / jnp.sum(e, axis=0, keepdims=True))).astype(BF16)
+        p = softmax(dot(k, q, (1, 0)), allowed)
         probs[h] = p
         mixed = dot(v, p, (1, 0)).astype(BF16)
         t_own[h % 2, h // 2] = dot(mixed, cot, (1, 0)).astype(BF16)
@@ -272,25 +300,31 @@
     diag_b.wait_recv()
     pass_b = w_push(8, w_rows(diagonal, CUT, pad - CUT), diagonal, other_core, CUT, pad - CUT)
     started += [pass_a, pass_b]
+    for copy in early:
+        copy.wait_recv()
+    for h in range(EARLY):
+        rows = pl.ds(h * pad, pad)
+        box_probs[h] = softmax(dot(early_in[1, rows], early_in[0, rows], (0, 0)), box_allowed)
     for copy in (w_c, pass_x, pass_y, pass_a, pass_b):
         copy.wait_recv()
     backs[...] = dot(w_all[...], cot, (1, 1)).astype(BF16)
+    back_out[...] = dot(backs[:ahead], pick, (1, 0)).astype(BF16)
+    ahead_back = e_push(3, back_out, back_in)
 
     boxes = []
-    for h in range(HEADS):
+    for at, h in enumerate(list(range(EARLY, HEADS)) + list(range(EARLY))):
         rows = pl.ds(h * pad, pad)
         q, k, v = qkv_ref[0, rows], qkv_ref[1, rows], nat_ref[2, :, h * pad:(h + 1) * pad]
         p, back = probs[h], backs[rows]
-        dp = dot(v, back, (1, 0))
-        pf = p.astype(F32)
-        ds = pf * (dp - jnp.sum(pf * dp, axis=0, keepdims=True))
-        ds = (ds * HSIZE ** (-0.5)).astype(BF16)
+        ds = score_grad(p, dot(v, back, (1, 0)))
         grads = (dot(k, ds, (1, 0)), dot(q, ds, (1, 1)), dot(back, p, (1, 1)))
         for i, grad in enumerate(grads):
             home_t[i, rows] = (grad * stay_row).astype(BF16)
-            box_out[i, h] = dot(grad.astype(BF16), pick, (1, 0)).astype(BF16)
-        boxes.append(push(box_out.at[:, h], box_in.at[:, h], b_send.at[h], b_recv.at[h], to_rank(lax.rem(rank + 1, n_dp))))
-        if h == 2:
+            if h >= EARLY:
+                box_out[i, at] = dot(grad.astype(BF16), pick, (1, 0)).astype(BF16)
+        if h >= EARLY:
+            boxes.append(push(box_out.at[:, at], box_in.at[:, h], b_send.at[at], b_recv.at[at], succ))
+        if at == 2:
             for i in range(2):
                 to_x[i].wait_recv()
                 x_mid[i] = (chip[2 * i + px, low].astype(F32) + x_first[i].astype(F32)).astype(BF16)
@@ -298,7 +332,7 @@
                 y_mid[i] = (chip[2 * py + i, high].astype(F32) + y_first[i].astype(F32)).astype(BF16)
             then_y = r_push(4, x_mid.at[1 - py], y_last, other_y)
             then_x = r_push(5, y_mid.at[1 - px], x_last, other_x)
-        if h == 5:
+        if at == 5:
             then_y.wait_recv()
             then_x.wait_recv()
             own_low = x_mid[py].astype(F32) + y_last[...].astype(F32)
@@ -313,6 +347,14 @@
                 target = lax.rem(rank + step, n_dp)
                 z_copies.append(push(z_out.at[target], z_in.at[step - 1], z_send.at[step - 1], z_recv.at[step - 1], to_rank(target)))
     started += boxes + z_copies
+    ahead_back.wait_recv()
+    for h in range(EARLY):
+        rows = pl.ds(h * pad, pad)
+        q, k, v, back, p = early_in[0, rows], early_in[1, rows], early_in[2, rows], back_in[rows], box_probs[h]
+        ds = score_grad(p, dot(v, back, (0, 0)))
+        box_in[0, h] = dot(k, ds, (1, 0)).astype(BF16)
+        box_in[1, h] = dot(q, ds, (1, 1)).astype(BF16)
+        box_in[2, h] = dot(back, p, (1, 1)).astype(BF16)
     for i in range(3):
         home_ref[i] = home_t[i].T
     total = z_out[rank].astype(F32)
@@ -354,6 +396,11 @@
             pltpu.VMEM((tok, dout), BF16),
             pltpu.VMEM((3, feats, tok), BF16),
             pltpu.VMEM((3, HEADS, pad, CLIP_MAX), BF16),
+            pltpu.VMEM((3, EARLY * pad, CLIP_MAX), BF16),
+            pltpu.VMEM((3, EARLY * pad, CLIP_MAX), BF16),
+            pltpu.VMEM((EARLY * pad, CLIP_MAX), BF16),
+            pltpu.VMEM((EARLY * pad, CLIP_MAX), BF16),
+            pltpu.VMEM((EARLY, CLIP_MAX, CLIP_MAX), BF16),
             pltpu.VMEM((feats, dout), BF16),
             pltpu.VMEM((HEADS, tok, tok), BF16),
             pltpu.VMEM((feats, tok), BF16),
@@ -368,8 +415,8 @@
             pltpu.VMEM((CUT, dout), BF16),
             pltpu.VMEM((n_dp, pad, width), BF16),
             pltpu.VMEM((n_dp - 1, pad, width), BF16),
-            pltpu.VMEM((3, HEADS, pad, CLIP_MAX), BF16),
-        ] + [pltpu.SemaphoreType.DMA((n,)) for n in (7, 9, 9, 4, 4, 6, 6, n_dp - 1, n_dp - 1, HEADS, HEADS)],
+            pltpu.VMEM((3, HEADS - EARLY, pad, CLIP_MAX), BF16),
+        ] + [pltpu.SemaphoreType.DMA((n,)) for n in (7, 9, 9, 4, 4, 6, 6, n_dp - 1, n_dp - 1, HEADS - EARLY, HEADS - EARLY, 4, 4)],
         compiler_params=pltpu.CompilerParams(
             collective_id=0, has_side_effects=True, vmem_limit_bytes=60 * 1024 * 1024
         ),

time: 46.1 us -> 39.6 us (0.86)
  Pallas kernels: 41.3 us -> 34.8 us
    pallas_call x1, Pallas kernels: 41.3 us -> 34.8 us  [fused(): pl.pallas_call(block_kernel, out_shape=(jax.ShapeDtypeStruct((3, tok, fea...]
where the time goes in v3:
time: 39.6 us; the launch traced here: 39.4 us
  Pallas kernels  34.8 us (88%)
  local copies, waits for them, and re-layouts  3.97 us (10%)
  between operations  0.65 us (2%)
    pallas_call x1, Pallas kernels, fused(): pl.pallas_call(block_kernel, out_shape=(jax.ShapeDtypeStruct((3, tok, fea...  34.8 us
    unnamed x7, local copies, waits for them, and re-layouts  3.97 us

profile of v3, /device:TPU:0, one launch (start us, length us, event | category | flops | bytes accessed | tf_op | source)
XLA Modules:
  0.0 39.4 jit_solution(3388817831622195536)
XLA Ops:
  0.6 34.8 %block.1 = (bf16[3,192,896]{2,1,0:T(8,128)(2,1)}, bf16[3,128,896]{2,1,0:T(8,128)(2,1)}, f32[112,224]{1,0:T(8,128)}) custom-call(s32[3,1,4]{2,1,0:T(1,128)} %bitcast.15, s32[1,2,3]{2,1,0:T(2,128)} %moves_hbm.1, bf16[3,192,896]{2,1,0:T(8,128)(2,1)} %bitcast.11, bf16[192,896]{1,0:T(8,128)(2,1)} %bitcast.14, bf16[112,896]{1,0:T(8,128)(2,1)} %w_ref.1), custom_call_target="tpu_custom_call" | custom-call | tf_op jit(solution)/shard_map/block/pallas_call | solution.py:382
  35.4 0.0 copy-start
  35.4 2.3 %copy.11 = bf16[1,1,192,3,896]{4,2,3,1,0:T(8,128)(2,1)} copy(bf16[1,1,192,3,896]{4,2,3,1,0:T(8,128)(2,1)} %bitcast.12) | data formatting | bytes 2064384
  37.8 0.0 copy-done
  37.8 0.0 copy-start.1
  37.8 0.8 %copy.12 = bf16[1,1,128,3,896]{4,2,3,1,0:T(8,128)(2,1)} copy(bf16[1,1,128,3,896]{4,2,3,1,0:T(8,128)(2,1)S(1)} %bitcast.13) | data formatting | bytes 1376256
  38.6 0.1 copy-done.1
  38.8 0.6 %copy.13 = f32[112,224]{1,0:T(8,128)} copy(f32[112,224]{1,0:T(8,128)S(1)} %copy-done.1) | data formatting | bytes 200704
Async XLA Ops:
  35.4 2.3 %copy-start = (bf16[3,128,896]{2,1,0:T(8,128)(2,1)S(1)}, bf16[3,128,896]{2,1,0:T(8,128)(2,1)}, u32[]{:S(2)}) copy-start(bf16[3,128,896]{2,1,0:T(8,128)(2,1)} %get-tuple-element.7) | copy-start | bytes 2064388
  37.8 1.0 %copy-start.1 = (f32[112,224]{1,0:T(8,128)S(1)}, f32[112,224]{1,0:T(8,128)}, u32[]{:S(2)}) copy-start(f32[112,224]{1,0:T(8,128)} %get-tuple-element.14) | copy-start | bytes 301060

commit v4 on v3

--- a/solution.py
+++ b/solution.py
@@ -139,9 +139,9 @@
 def block_kernel(
     lens_hbm, moves_hbm, qkv_hbm, g_hbm, w_ref,
     home_ref, box_ref, wg_ref,
-    lens_ref, moves_ref, nat_ref, qkv_ref, g_ref, home_t, box_in, early_out, early_in, back_out, back_in, box_probs, w_all, probs, backs, t_own, t_core, chip, x_first, y_first, x_mid, y_mid, x_last, y_last,
+    home_nat, box_nat, wg_own, lens_ref, moves_ref, nat_ref, qkv_ref, g_ref, home_t, box_in, early_out, early_in, back_out, back_in, box_probs, w_all, probs, backs, t_own, t_core, chip, x_first, y_first, x_mid, y_mid, x_last, y_last,
     z_out, z_in, box_out,
-    in_sem, w_send, w_recv, c_send, c_recv, r_send, r_recv, z_send, z_recv, b_send, b_recv, e_send, e_recv,
+    in_sem, out_sem, w_send, w_recv, c_send, c_recv, r_send, r_recv, z_send, z_recv, b_send, b_recv, e_send, e_recv,
 ):
     rank, col = lax.axis_index("dp"), lax.axis_index("fsdp")
     core = lax.rem(col, 2)
@@ -176,6 +176,13 @@
     ]
     for fetch in fetches:
         fetch.start()
+    left = []
+
+    def leave(slot, src, dst):
+        copy = pltpu.make_async_copy(src, dst, out_sem.at[slot])
+        copy.start()
+        left.append(copy)
+
     barrier = pltpu.get_barrier_semaphore()
     partners = [to_col(other_core), to_col(other_x), to_col(other_y)]
     partners += [to_rank(lax.rem(rank + k, n_dp)) for k in range(1, n_dp)]
@@ -269,11 +276,14 @@
         p = softmax(dot(k, q, (1, 0)), allowed)
         probs[h] = p
         mixed = dot(v, p, (1, 0)).astype(BF16)
-        t_own[h % 2, h // 2] = dot(mixed, cot, (1, 0)).astype(BF16)
-        if h % 2 == 1:
+        if h % 2 == 0:
+            even = mixed
+        else:
             m = h // 2
+            term = dot(jnp.concatenate([even, mixed], axis=0), cot, (1, 0)).astype(BF16)
+            t_own[0, m], t_own[1, m] = term[:pad], term[pad:]
             c_copies.append(push(t_own.at[1 - core, m], t_core.at[m], c_send.at[m], c_recv.at[m], to_col(other_core)))
-        if h == 3:
+        if h == 1:
             w_x.wait_recv()
             diag_a = w_push(3, w_rows(other_x, 0, CUT), other_x, other_y, 0, CUT)
             pass_x = w_push(5, w_rows(other_x), other_x, other_core)
@@ -281,12 +291,24 @@
             diag_b = w_push(4, w_rows(other_y, CUT, pad - CUT), other_y, other_x, CUT, pad - CUT)
             pass_y = w_push(6, w_rows(other_y), other_y, other_core)
             started += [diag_a, pass_x, diag_b, pass_y]
+        if h == 5:
+            diag_a.wait_recv()
+            pass_a = w_push(7, w_rows(diagonal, 0, CUT), diagonal, other_core, 0, CUT)
+            diag_b.wait_recv()
+            pass_b = w_push(8, w_rows(diagonal, CUT, pad - CUT), diagonal, other_core, CUT, pad - CUT)
+            started += [pass_a, pass_b]
     started += c_copies
 
     def r_push(slot, src, dst, target):
         copy = push(src, dst, r_send.at[slot], r_recv.at[slot], to_col(target))
         started.append(copy)
         return copy
+
+    for copy in (w_c, pass_x, pass_y, pass_a, pass_b):
+        copy.wait_recv()
+    backs[...] = dot(w_all[...], cot, (1, 1)).astype(BF16)
+    back_out[...] = dot(backs[:ahead], pick, (1, 0)).astype(BF16)
+    ahead_back = e_push(3, back_out, back_in)
 
     low, high = pl.ds(0, CUT), pl.ds(CUT, pad - CUT)
     for m in range(4):
@@ -294,22 +316,6 @@
         chip[m] = (t_own[core, m].astype(F32) + t_core[m].astype(F32)).astype(BF16)
     to_x = [r_push(i, chip.at[2 * i + 1 - px, low], x_first.at[i], other_x) for i in range(2)]
     to_y = [r_push(2 + i, chip.at[2 * (1 - py) + i, high], y_first.at[i], other_y) for i in range(2)]
-
-    diag_a.wait_recv()
-    pass_a = w_push(7, w_rows(diagonal, 0, CUT), diagonal, other_core, 0, CUT)
-    diag_b.wait_recv()
-    pass_b = w_push(8, w_rows(diagonal, CUT, pad - CUT), diagonal, other_core, CUT, pad - CUT)
-    started += [pass_a, pass_b]
-    for copy in early:
-        copy.wait_recv()
-    for h in range(EARLY):
-        rows = pl.ds(h * pad, pad)
-        box_probs[h] = softmax(dot(early_in[1, rows], early_in[0, rows], (0, 0)), box_allowed)
-    for copy in (w_c, pass_x, pass_y, pass_a, pass_b):
-        copy.wait_recv()
-    backs[...] = dot(w_all[...], cot, (1, 1)).astype(BF16)
-    back_out[...] = dot(backs[:ahead], pick, (1, 0)).astype(BF16)
-    ahead_back = e_push(3, back_out, back_in)
 
     boxes = []
     for at, h in enumerate(list(range(EARLY, HEADS)) + list(range(EARLY))):
@@ -318,13 +324,20 @@
         p, back = probs[h], backs[rows]
         ds = score_grad(p, dot(v, back, (1, 0)))
         grads = (dot(k, ds, (1, 0)), dot(q, ds, (1, 1)), dot(back, p, (1, 1)))
+        if h >= EARLY:
+            picked_grads = dot(jnp.concatenate([grad.astype(BF16) for grad in grads], axis=0), pick, (1, 0))
+            for i in range(3):
+                box_out[i, at] = picked_grads[i * pad:(i + 1) * pad].astype(BF16)
+            boxes.append(push(box_out.at[:, at], box_in.at[:, h], b_send.at[at], b_recv.at[at], succ))
         for i, grad in enumerate(grads):
             home_t[i, rows] = (grad * stay_row).astype(BF16)
-            if h >= EARLY:
-                box_out[i, at] = dot(grad.astype(BF16), pick, (1, 0)).astype(BF16)
-        if h >= EARLY:
-            boxes.append(push(box_out.at[:, at], box_in.at[:, h], b_send.at[at], b_recv.at[at], succ))
-        if at == 2:
+        if at == HEADS - EARLY - 1:
+            for copy in early:
+                copy.wait_recv()
+            for b in range(EARLY):
+                rows = pl.ds(b * pad, pad)
+                box_probs[b] = softmax(dot(early_in[1, rows], early_in[0, rows], (0, 0)), box_allowed)
+        if at == 4:
             for i in range(2):
                 to_x[i].wait_recv()
                 x_mid[i] = (chip[2 * i + px, low].astype(F32) + x_first[i].astype(F32)).astype(BF16)
@@ -332,7 +345,7 @@
                 y_mid[i] = (chip[2 * py + i, high].astype(F32) + y_first[i].astype(F32)).astype(BF16)
             then_y = r_push(4, x_mid.at[1 - py], y_last, other_y)
             then_x = r_push(5, y_mid.at[1 - px], x_last, other_x)
-        if at == 5:
+        if at == 7:
             then_y.wait_recv()
             then_x.wait_recv()
             own_low = x_mid[py].astype(F32) + y_last[...].astype(F32)
@@ -347,6 +360,9 @@
                 target = lax.rem(rank + step, n_dp)
                 z_copies.append(push(z_out.at[target], z_in.at[step - 1], z_send.at[step - 1], z_recv.at[step - 1], to_rank(target)))
     started += boxes + z_copies
+    for i in range(3):
+        home_nat[i] = home_t[i].T
+        leave(i, home_nat.at[i], home_ref.at[i])
     ahead_back.wait_recv()
     for h in range(EARLY):
         rows = pl.ds(h * pad, pad)
@@ -355,19 +371,36 @@
         box_in[0, h] = dot(k, ds, (1, 0)).astype(BF16)
         box_in[1, h] = dot(q, ds, (1, 1)).astype(BF16)
         box_in[2, h] = dot(back, p, (1, 1)).astype(BF16)
-    for i in range(3):
-        home_ref[i] = home_t[i].T
     total = z_out[rank].astype(F32)
     for step, copy in enumerate(z_copies):
         copy.wait_recv()
         total += z_in[step].astype(F32)
-    wg_ref[...] = total
+    wg_own[...] = total
+    leave(6, wg_own, wg_ref)
     for copy in boxes:
         copy.wait_recv()
     for i in range(3):
-        box_ref[i] = box_in[i].reshape(HEADS * pad, CLIP_MAX).T
+        box_nat[i] = box_in[i].reshape(HEADS * pad, CLIP_MAX).T
+        leave(3 + i, box_nat.at[i], box_ref.at[i])
+    for copy in left:
+        copy.wait()
     for copy in started:
         copy.wait_send()
+
+
+def hand_out(home, box, weight, home_to, box_to, weight_to, sem):
+    copies = []
+    for src, dst in ((home, home_to), (box, box_to)):
+        half = src.shape[1] // 2
+        for i in range(3):
+            for begin in (0, half):
+                at = (i, pl.ds(begin, half))
+                copies.append(pltpu.make_async_copy(src.at[at], dst.at[at], sem.at[len(copies)]))
+    copies.append(pltpu.make_async_copy(weight, weight_to, sem.at[len(copies)]))
+    for copy in copies:
+        copy.start()
+    for copy in copies:
+        copy.wait()
 
 
 def fused(qkv, grad_out, lengths, moves, out_weight):
@@ -375,20 +408,23 @@
     tok, feats = qkv.shape[2], qkv.shape[4]
     dout = grad_out.shape[3]
     pad, rest, width = HSIZE, HSIZE - CUT, dout // n_dp
-    vmem = pl.BlockSpec(memory_space=pltpu.VMEM)
     hbm = pl.BlockSpec(memory_space=pltpu.HBM)
     natural = jnp.transpose(qkv[0, 0], (1, 0, 2))
     by_clip = jnp.transpose(lengths, (2, 1, 0))
-    home, box, weight_grad = pl.pallas_call(
+    results = (
+        jax.ShapeDtypeStruct((3, tok, feats), BF16),
+        jax.ShapeDtypeStruct((3, CLIP_MAX, feats), BF16),
+        jax.ShapeDtypeStruct((pad, width), F32),
+    )
+    made = pl.pallas_call(
         block_kernel,
-        out_shape=(
-            jax.ShapeDtypeStruct((3, tok, feats), BF16),
-            jax.ShapeDtypeStruct((3, CLIP_MAX, feats), BF16),
-            jax.ShapeDtypeStruct((pad, width), F32),
-        ),
+        out_shape=results,
         in_specs=[hbm] * 5,
-        out_specs=(vmem, vmem, vmem),
+        out_specs=(hbm, hbm, hbm),
         scratch_shapes=[
+            pltpu.VMEM((3, tok, feats), BF16),
+            pltpu.VMEM((3, CLIP_MAX, feats), BF16),
+            pltpu.VMEM((pad, width), F32),
             pltpu.SMEM(by_clip.shape, jnp.int32),
             pltpu.SMEM(moves.shape, jnp.int32),
             pltpu.VMEM((3, tok, feats), BF16),
@@ -416,12 +452,21 @@
             pltpu.VMEM((n_dp, pad, width), BF16),
             pltpu.VMEM((n_dp - 1, pad, width), BF16),
             pltpu.VMEM((3, HEADS - EARLY, pad, CLIP_MAX), BF16),
-        ] + [pltpu.SemaphoreType.DMA((n,)) for n in (7, 9, 9, 4, 4, 6, 6, n_dp - 1, n_dp - 1, HEADS - EARLY, HEADS - EARLY, 4, 4)],
+        ] + [pltpu.SemaphoreType.DMA((n,)) for n in (7, 7, 9, 9, 4, 4, 6, 6, n_dp - 1, n_dp - 1, HEADS - EARLY, HEADS - EARLY, 4, 4)],
         compiler_params=pltpu.CompilerParams(
             collective_id=0, has_side_effects=True, vmem_limit_bytes=60 * 1024 * 1024
         ),
         name="block",
     )(by_clip, moves, natural, grad_out[0, 0], out_weight)
+    home, box, weight_grad = pl.pallas_call(
+        hand_out,
+        out_shape=results,
+        in_specs=[hbm] * 3,
+        out_specs=(hbm,) * 3,
+        scratch_shapes=[pltpu.SemaphoreType.DMA((13,))],
+        compiler_params=pltpu.CompilerParams(vmem_limit_bytes=60 * 1024 * 1024),
+        name="hand_out",
+    )(*made)
     home_grad = jnp.transpose(home, (1, 0, 2))
     inbox_grad = jnp.transpose(box, (1, 0, 2))
     return (home_grad[None, None], inbox_grad[None, None], weight_grad)

time: 39.6 us -> 93.5 us (2.36)
  Pallas kernels: 34.8 us -> 92.7 us
  local copies, waits for them, and re-layouts: 3.97 us -> 0 us
    pallas_call x1 -> x2, Pallas kernels: 34.8 us -> 92.7 us  [the longest x1 56.8 us: fused(): pl.pallas_call(hand_out, out_shape=results, in_specs=[hbm] * 3, out_specs...]
    unnamed x7 -> x0, local copies, waits for them, and re-layouts: 3.97 us -> none
where the time goes in v4:
time: 93.5 us; the launch traced here: 93.4 us
  Pallas kernels  92.7 us (99%)
    pallas_call x1, Pallas kernels, fused(): pl.pallas_call(hand_out, out_shape=results, in_specs=[hbm] * 3, out_specs...  56.8 us
    pallas_call x1, Pallas kernels, fused(): pl.pallas_call(block_kernel, out_shape=results, in_specs=[hbm] * 5, out_s...  35.9 us

profile of v4, /device:TPU:0, one launch (start us, length us, event | category | flops | bytes accessed | tf_op | source)
XLA Modules:
  0.0 93.4 jit_solution(17902154295206917514)
XLA Ops:
  0.6 35.9 %block.1 = (bf16[3,192,896]{2,1,0:T(8,128)(2,1)}, bf16[3,128,896]{2,1,0:T(8,128)(2,1)}, f32[112,224]{1,0:T(8,128)}) custom-call(s32[3,1,4]{2,1,0:T(1,128)} %bitcast.13, s32[1,2,3]{2,1,0:T(2,128)} %moves_hbm.1, bf16[3,192,896]{2,1,0:T(8,128)(2,1)} %bitcast.11, bf16[192,896]{1,0:T(8,128)(2,1)} %bitcast.12, bf16[112,896]{1,0:T(8,128)(2,1)} %w_ref.1), custom_call_target="tpu_custom_call" | custom-call | tf_op jit(solution)/shard_map/block/pallas_call | solution.py:419
  36.5 56.8 %hand_out.1 = (bf16[3,192,896]{2,1,0:T(8,128)(2,1)}, bf16[3,128,896]{2,1,0:T(8,128)(2,1)}, f32[112,224]{1,0:T(8,128)}) custom-call(bf16[3,192,896]{2,1,0:T(8,128)(2,1)} %get-tuple-element.9.home, bf16[3,128,896]{2,1,0:T(8,128)(2,1)} %get-tuple-element.10.box, f32[112,224]{1,0:T(8,128)} %get-tuple-element.11.weight), custom_call_target="tpu_custom_call" | custom-call | tf_op jit(solution)/shard_map/hand_out/pallas_call | solution.py:461

commit v5 on v3

--- a/solution.py
+++ b/solution.py
@@ -263,17 +263,20 @@
 
     cot = g_ref[...]
     c_copies = []
-    for h in range(HEADS):
-        rows = pl.ds(h * pad, pad)
-        q, k, v = qkv_ref[0, rows], nat_ref[1, :, h * pad:(h + 1) * pad], qkv_ref[2, rows]
-        p = softmax(dot(k, q, (1, 0)), allowed)
-        probs[h] = p
-        mixed = dot(v, p, (1, 0)).astype(BF16)
-        t_own[h % 2, h // 2] = dot(mixed, cot, (1, 0)).astype(BF16)
-        if h % 2 == 1:
-            m = h // 2
+    for group in range(2):
+        heads = [4 * group + i for i in range(4)]
+        rows = [pl.ds(h * pad, pad) for h in heads]
+        scores = [dot(nat_ref[1, :, h * pad:(h + 1) * pad], qkv_ref[0, rs], (1, 0)) for h, rs in zip(heads, rows)]
+        ps = [softmax(each, allowed) for each in scores]
+        mixed = [dot(qkv_ref[2, rs], p, (1, 0)).astype(BF16) for p, rs in zip(ps, rows)]
+        for h, p in zip(heads, ps):
+            probs[h] = p
+        term = dot(jnp.concatenate(mixed, axis=0), cot, (1, 0)).astype(BF16)
+        for i, h in enumerate(heads):
+            t_own[h % 2, h // 2] = term[i * pad:(i + 1) * pad]
+        for m in (2 * group, 2 * group + 1):
             c_copies.append(push(t_own.at[1 - core, m], t_core.at[m], c_send.at[m], c_recv.at[m], to_col(other_core)))
-        if h == 3:
+        if group == 0:
             w_x.wait_recv()
             diag_a = w_push(3, w_rows(other_x, 0, CUT), other_x, other_y, 0, CUT)
             pass_x = w_push(5, w_rows(other_x), other_x, other_core)
@@ -300,63 +303,77 @@
     diag_b.wait_recv()
     pass_b = w_push(8, w_rows(diagonal, CUT, pad - CUT), diagonal, other_core, CUT, pad - CUT)
     started += [pass_a, pass_b]
-    for copy in early:
-        copy.wait_recv()
-    for h in range(EARLY):
-        rows = pl.ds(h * pad, pad)
-        box_probs[h] = softmax(dot(early_in[1, rows], early_in[0, rows], (0, 0)), box_allowed)
     for copy in (w_c, pass_x, pass_y, pass_a, pass_b):
         copy.wait_recv()
     backs[...] = dot(w_all[...], cot, (1, 1)).astype(BF16)
     back_out[...] = dot(backs[:ahead], pick, (1, 0)).astype(BF16)
     ahead_back = e_push(3, back_out, back_in)
 
+    def home_group(heads):
+        rows = [pl.ds(h * pad, pad) for h in heads]
+        ps = [probs[h] for h in heads]
+        dps = [dot(nat_ref[2, :, h * pad:(h + 1) * pad], backs[rs], (1, 0)) for h, rs in zip(heads, rows)]
+        dss = [score_grad(p, dp) for p, dp in zip(ps, dps)]
+        grads = [
+            (dot(qkv_ref[1, rs], ds, (1, 0)), dot(qkv_ref[0, rs], ds, (1, 1)), dot(backs[rs], p, (1, 1)))
+            for rs, ds, p in zip(rows, dss, ps)
+        ]
+        for rs, each in zip(rows, grads):
+            for i in range(3):
+                home_t[i, rs] = (each[i] * stay_row).astype(BF16)
+        return grads
+
+    late = list(range(EARLY, HEADS))
+    flat = [grad.astype(BF16) for each in home_group(late) for grad in each]
+    picked_grads = dot(jnp.concatenate(flat, axis=0), pick, (1, 0)).astype(BF16)
     boxes = []
-    for at, h in enumerate(list(range(EARLY, HEADS)) + list(range(EARLY))):
-        rows = pl.ds(h * pad, pad)
-        q, k, v = qkv_ref[0, rows], qkv_ref[1, rows], nat_ref[2, :, h * pad:(h + 1) * pad]
-        p, back = probs[h], backs[rows]
-        ds = score_grad(p, dot(v, back, (1, 0)))
-        grads = (dot(k, ds, (1, 0)), dot(q, ds, (1, 1)), dot(back, p, (1, 1)))
-        for i, grad in enumerate(grads):
-            home_t[i, rows] = (grad * stay_row).astype(BF16)
-            if h >= EARLY:
-                box_out[i, at] = dot(grad.astype(BF16), pick, (1, 0)).astype(BF16)
-        if h >= EARLY:
-            boxes.append(push(box_out.at[:, at], box_in.at[:, h], b_send.at[at], b_recv.at[at], succ))
-        if at == 2:
-            for i in range(2):
-                to_x[i].wait_recv()
-                x_mid[i] = (chip[2 * i + px, low].astype(F32) + x_first[i].astype(F32)).astype(BF16)
-                to_y[i].wait_recv()
-                y_mid[i] = (chip[2 * py + i, high].astype(F32) + y_first[i].astype(F32)).astype(BF16)
-            then_y = r_push(4, x_mid.at[1 - py], y_last, other_y)
-            then_x = r_push(5, y_mid.at[1 - px], x_last, other_x)
-        if at == 5:
-            then_y.wait_recv()
-            then_x.wait_recv()
-            own_low = x_mid[py].astype(F32) + y_last[...].astype(F32)
-            own_high = y_mid[px].astype(F32) + x_last[...].astype(F32)
-            width = z_out.shape[2]
-            for part in range(n_dp):
-                cut = slice(part * width, (part + 1) * width)
-                z_out[part, low] = own_low[:, cut].astype(BF16)
-                z_out[part, high] = own_high[:, cut].astype(BF16)
-            z_copies = []
-            for step in range(1, n_dp):
-                target = lax.rem(rank + step, n_dp)
-                z_copies.append(push(z_out.at[target], z_in.at[step - 1], z_send.at[step - 1], z_recv.at[step - 1], to_rank(target)))
+    for at, h in enumerate(late):
+        for i in range(3):
+            begin = (3 * at + i) * pad
+            box_out[i, at] = picked_grads[begin:begin + pad]
+        boxes.append(push(box_out.at[:, at], box_in.at[:, h], b_send.at[at], b_recv.at[at], succ))
+
+    for copy in early:
+        copy.wait_recv()
+    clip_rows = [pl.ds(h * pad, pad) for h in range(EARLY)]
+    clip_scores = [dot(early_in[1, rs], early_in[0, rs], (0, 0)) for rs in clip_rows]
+    for h, each in enumerate(clip_scores):
+        box_probs[h] = softmax(each, box_allowed)
+
+    for i in range(2):
+        to_x[i].wait_recv()
+        x_mid[i] = (chip[2 * i + px, low].astype(F32) + x_first[i].astype(F32)).astype(BF16)
+        to_y[i].wait_recv()
+        y_mid[i] = (chip[2 * py + i, high].astype(F32) + y_first[i].astype(F32)).astype(BF16)
+    then_y = r_push(4, x_mid.at[1 - py], y_last, other_y)
+    then_x = r_push(5, y_mid.at[1 - px], x_last, other_x)
+
+    home_group(list(range(EARLY)))
+
+    then_y.wait_recv()
+    then_x.wait_recv()
+    own_low = x_mid[py].astype(F32) + y_last[...].astype(F32)
+    own_high = y_mid[px].astype(F32) + x_last[...].astype(F32)
+    width = z_out.shape[2]
+    for part in range(n_dp):
+        cut = slice(part * width, (part + 1) * width)
+        z_out[part, low] = own_low[:, cut].astype(BF16)
+        z_out[part, high] = own_high[:, cut].astype(BF16)
+    z_copies = []
+    for step in range(1, n_dp):
+        target = lax.rem(rank + step, n_dp)
+        z_copies.append(push(z_out.at[target], z_in.at[step - 1], z_send.at[step - 1], z_recv.at[step - 1], to_rank(target)))
     started += boxes + z_copies
-    ahead_back.wait_recv()
-    for h in range(EARLY):
-        rows = pl.ds(h * pad, pad)
-        q, k, v, back, p = early_in[0, rows], early_in[1, rows], early_in[2, rows], back_in[rows], box_probs[h]
-        ds = score_grad(p, dot(v, back, (0, 0)))
-        box_in[0, h] = dot(k, ds, (1, 0)).astype(BF16)
-        box_in[1, h] = dot(q, ds, (1, 1)).astype(BF16)
-        box_in[2, h] = dot(back, p, (1, 1)).astype(BF16)
+
     for i in range(3):
         home_ref[i] = home_t[i].T
+    ahead_back.wait_recv()
+    dps = [dot(early_in[2, rs], back_in[rs], (0, 0)) for rs in clip_rows]
+    dss = [score_grad(box_probs[h], dps[h]) for h in range(EARLY)]
+    for h, rs in enumerate(clip_rows):
+        box_in[0, h] = dot(early_in[1, rs], dss[h], (1, 0)).astype(BF16)
+        box_in[1, h] = dot(early_in[0, rs], dss[h], (1, 1)).astype(BF16)
+        box_in[2, h] = dot(back_in[rs], box_probs[h], (1, 1)).astype(BF16)
     total = z_out[rank].astype(F32)
     for step, copy in enumerate(z_copies):
         copy.wait_recv()
@@ -370,24 +387,40 @@
         copy.wait_send()
 
 
+def hand_out(home, box, weight, home_to, box_to, weight_to, sem):
+    copies = []
+    for src, dst in ((home, home_to), (box, box_to)):
+        half = src.shape[1] // 2
+        for i in range(3):
+            for begin in (0, half):
+                at = (i, pl.ds(begin, half))
+                copies.append(pltpu.make_async_copy(src.at[at], dst.at[at], sem.at[len(copies)]))
+    copies.append(pltpu.make_async_copy(weight, weight_to, sem.at[len(copies)]))
+    for copy in copies:
+        copy.start()
+    for copy in copies:
+        copy.wait()
+
+
 def fused(qkv, grad_out, lengths, moves, out_weight):
     n_dp = lax.axis_size("dp")
     tok, feats = qkv.shape[2], qkv.shape[4]
     dout = grad_out.shape[3]
     pad, rest, width = HSIZE, HSIZE - CUT, dout // n_dp
-    vmem = pl.BlockSpec(memory_space=pltpu.VMEM)
     hbm = pl.BlockSpec(memory_space=pltpu.HBM)
     natural = jnp.transpose(qkv[0, 0], (1, 0, 2))
     by_clip = jnp.transpose(lengths, (2, 1, 0))
-    home, box, weight_grad = pl.pallas_call(
+    vmem = pl.BlockSpec(memory_space=pltpu.VMEM)
+    results = (
+        jax.ShapeDtypeStruct((3, tok, feats), BF16),
+        jax.ShapeDtypeStruct((3, CLIP_MAX, feats), BF16),
+        jax.ShapeDtypeStruct((pad, width), F32),
+    )
+    made = pl.pallas_call(
         block_kernel,
-        out_shape=(
-            jax.ShapeDtypeStruct((3, tok, feats), BF16),
-            jax.ShapeDtypeStruct((3, CLIP_MAX, feats), BF16),
-            jax.ShapeDtypeStruct((pad, width), F32),
-        ),
+        out_shape=tuple(pltpu.VMEM(each.shape, each.dtype) for each in results),
         in_specs=[hbm] * 5,
-        out_specs=(vmem, vmem, vmem),
+        out_specs=(vmem,) * 3,
         scratch_shapes=[
             pltpu.SMEM(by_clip.shape, jnp.int32),
             pltpu.SMEM(moves.shape, jnp.int32),
@@ -422,6 +455,15 @@
         ),
         name="block",
     )(by_clip, moves, natural, grad_out[0, 0], out_weight)
+    home, box, weight_grad = pl.pallas_call(
+        hand_out,
+        out_shape=results,
+        in_specs=[vmem] * 3,
+        out_specs=(hbm,) * 3,
+        scratch_shapes=[pltpu.SemaphoreType.DMA((13,))],
+        compiler_params=pltpu.CompilerParams(vmem_limit_bytes=8 * 1024 * 1024),
+        name="hand_out",
+    )(*made)
     home_grad = jnp.transpose(home, (1, 0, 2))
     inbox_grad = jnp.transpose(box, (1, 0, 2))
     return (home_grad[None, None], inbox_grad[None, None], weight_grad)

time: 39.6 us -> 34.8 us (0.88)
  local copies, waits for them, and re-layouts: 3.97 us -> 0 us
  Pallas kernels: 34.8 us -> 34.1 us
    unnamed x7 -> x0, local copies, waits for them, and re-layouts: 3.97 us -> none
    pallas_call x1 -> x2, Pallas kernels: 34.8 us -> 34.1 us  [the longest x1 32.7 us: fused(): pl.pallas_call(block_kernel, out_shape=tuple((pltpu.VMEM(each.shape, each...]
where the time goes in v5:
time: 34.8 us; the launch traced here: 34.7 us
  Pallas kernels  34.1 us (98%)
  between operations  0.64 us (2%)
    pallas_call x1, Pallas kernels, fused(): pl.pallas_call(block_kernel, out_shape=tuple((pltpu.VMEM(each.shape, each...  32.7 us
    pallas_call x1, Pallas kernels, fused(): pl.pallas_call(hand_out, out_shape=results, in_specs=[vmem] * 3, out_spec...  1.33 us

profile of v5, /device:TPU:0, one launch (start us, length us, event | category | flops | bytes accessed | tf_op | source)
XLA Modules:
  0.0 34.7 jit_solution(9065418916627142041)
XLA Ops:
  0.6 32.7 %block.1 = (bf16[3,192,896]{2,1,0:T(8,128)(2,1)S(1)}, bf16[3,128,896]{2,1,0:T(8,128)(2,1)S(1)}, f32[112,224]{1,0:T(8,128)S(1)}) custom-call(s32[3,1,4]{2,1,0:T(1,128)} %bitcast.13, s32[1,2,3]{2,1,0:T(2,128)} %moves_hbm.1, bf16[3,192,896]{2,1,0:T(8,128)(2,1)} %bitcast.11, bf16[192,896]{1,0:T(8,128)(2,1)} %bitcast.12, bf16[112,896]{1,0:T(8,128)(2,1)} %w_ref.1), custom_call_target="tpu_custom_call" | custom-call | tf_op jit(solution)/shard_map/block/pallas_call | solution.py:419
  33.4 1.3 %hand_out.1 = (bf16[3,192,896]{2,1,0:T(8,128)(2,1)}, bf16[3,128,896]{2,1,0:T(8,128)(2,1)}, f32[112,224]{1,0:T(8,128)}) custom-call(bf16[3,192,896]{2,1,0:T(8,128)(2,1)S(1)} %get-tuple-element.9.home, bf16[3,128,896]{2,1,0:T(8,128)(2,1)S(1)} %get-tuple-element.10.box, f32[112,224]{1,0:T(8,128)S(1)} %get-tuple-element.11.weight), custom_call_target="tpu_custom_call" | custom-call | tf_op jit(solution)/shard_map/hand_out/pallas_call | solution.py:458

commit v6 on v5

--- a/solution.py
+++ b/solution.py
@@ -190,14 +190,15 @@
         return push(src, w_rows(owner, begin, count), w_send.at[slot], w_recv.at[slot], to_col(target))
 
     started = []
-    w_x = w_push(0, w_ref, col, other_x)
-    w_y = w_push(1, w_ref, col, other_y)
+    rest = pad - CUT
+    w_x = w_push(0, w_ref.at[pl.ds(0, CUT)], col, other_x, 0, CUT)
+    w_y = w_push(1, w_ref.at[pl.ds(CUT, rest)], col, other_y, CUT, rest)
+    w_x_rest = w_push(9, w_ref.at[pl.ds(CUT, rest)], col, other_x, CUT, rest)
+    w_y_rest = w_push(10, w_ref.at[pl.ds(0, CUT)], col, other_y, 0, CUT)
     w_c = w_push(2, w_ref, col, other_core)
-    started += [w_x, w_y, w_c]
-    for fetch in fetches:
+    started += [w_x, w_y, w_x_rest, w_y_rest, w_c]
+    for fetch in fetches[:2]:
         fetch.wait()
-    for i in range(3):
-        qkv_ref[i] = nat_ref[i].T
 
     l0, l1, l2 = lens_ref[0, 0, rank], lens_ref[1, 0, rank], lens_ref[2, 0, rank]
     e0, e1 = l0, l0 + l1
@@ -240,6 +241,8 @@
 
     early = []
     for i in range(3):
+        fetches[2 + i].wait()
+        qkv_ref[i] = nat_ref[i].T
         early_out[i] = dot(qkv_ref[i, :ahead], pick, (1, 0)).astype(BF16)
         early.append(e_push(i, early_out.at[i], early_in.at[i]))
 
@@ -261,6 +264,8 @@
         ds = pf * (dp - jnp.sum(pf * dp, axis=0, keepdims=True))
         return (ds * HSIZE ** (-0.5)).astype(BF16)
 
+    for fetch in fetches[5:]:
+        fetch.wait()
     cot = g_ref[...]
     c_copies = []
     for group in range(2):
@@ -279,11 +284,14 @@
         if group == 0:
             w_x.wait_recv()
             diag_a = w_push(3, w_rows(other_x, 0, CUT), other_x, other_y, 0, CUT)
-            pass_x = w_push(5, w_rows(other_x), other_x, other_core)
             w_y.wait_recv()
-            diag_b = w_push(4, w_rows(other_y, CUT, pad - CUT), other_y, other_x, CUT, pad - CUT)
-            pass_y = w_push(6, w_rows(other_y), other_y, other_core)
-            started += [diag_a, pass_x, diag_b, pass_y]
+            diag_b = w_push(4, w_rows(other_y, CUT, rest), other_y, other_x, CUT, rest)
+            started += [diag_a, diag_b]
+    w_x_rest.wait_recv()
+    pass_x = w_push(5, w_rows(other_x), other_x, other_core)
+    w_y_rest.wait_recv()
+    pass_y = w_push(6, w_rows(other_y), other_y, other_core)
+    started += [pass_x, pass_y]
     started += c_copies
 
     def r_push(slot, src, dst, target):
@@ -374,15 +382,15 @@
         box_in[0, h] = dot(early_in[1, rs], dss[h], (1, 0)).astype(BF16)
         box_in[1, h] = dot(early_in[0, rs], dss[h], (1, 1)).astype(BF16)
         box_in[2, h] = dot(back_in[rs], box_probs[h], (1, 1)).astype(BF16)
+    for copy in boxes:
+        copy.wait_recv()
+    for i in range(3):
+        box_ref[i] = box_in[i].reshape(HEADS * pad, CLIP_MAX).T
     total = z_out[rank].astype(F32)
     for step, copy in enumerate(z_copies):
         copy.wait_recv()
         total += z_in[step].astype(F32)
     wg_ref[...] = total
-    for copy in boxes:
-        copy.wait_recv()
-    for i in range(3):
-        box_ref[i] = box_in[i].reshape(HEADS * pad, CLIP_MAX).T
     for copy in started:
         copy.wait_send()
 
@@ -449,7 +457,7 @@
             pltpu.VMEM((n_dp, pad, width), BF16),
             pltpu.VMEM((n_dp - 1, pad, width), BF16),
             pltpu.VMEM((3, HEADS - EARLY, pad, CLIP_MAX), BF16),
-        ] + [pltpu.SemaphoreType.DMA((n,)) for n in (7, 9, 9, 4, 4, 6, 6, n_dp - 1, n_dp - 1, HEADS - EARLY, HEADS - EARLY, 4, 4)],
+        ] + [pltpu.SemaphoreType.DMA((n,)) for n in (7, 11, 11, 4, 4, 6, 6, n_dp - 1, n_dp - 1, HEADS - EARLY, HEADS - EARLY, 4, 4)],
         compiler_params=pltpu.CompilerParams(
             collective_id=0, has_side_effects=True, vmem_limit_bytes=60 * 1024 * 1024
         ),

time: 34.8 us -> 34 us (0.977)
  Pallas kernels: 34.1 us -> 33.2 us
    pallas_call x1, Pallas kernels: 32.7 us -> 31.8 us  [fused(): pl.pallas_call(block_kernel, out_shape=tuple((pltpu.VMEM(each.shape, each...]
where the time goes in v6:
time: 34 us; the launch traced here: 33.8 us
  Pallas kernels  33.2 us (98%)
  between operations  0.64 us (2%)
    pallas_call x1, Pallas kernels, fused(): pl.pallas_call(block_kernel, out_shape=tuple((pltpu.VMEM(each.shape, each...  31.8 us
    pallas_call x1, Pallas kernels, fused(): pl.pallas_call(hand_out, out_shape=results, in_specs=[vmem] * 3, out_spec...  1.33 us

profile of v6, /device:TPU:0, one launch (start us, length us, event | category | flops | bytes accessed | tf_op | source)
XLA Modules:
  0.0 33.8 jit_solution(2843711322590182185)
XLA Ops:
  0.6 31.8 %block.1 = (bf16[3,192,896]{2,1,0:T(8,128)(2,1)S(1)}, bf16[3,128,896]{2,1,0:T(8,128)(2,1)S(1)}, f32[112,224]{1,0:T(8,128)S(1)}) custom-call(s32[3,1,4]{2,1,0:T(1,128)} %bitcast.13, s32[1,2,3]{2,1,0:T(2,128)} %moves_hbm.1, bf16[3,192,896]{2,1,0:T(8,128)(2,1)} %bitcast.11, bf16[192,896]{1,0:T(8,128)(2,1)} %bitcast.12, bf16[112,896]{1,0:T(8,128)(2,1)} %w_ref.1), custom_call_target="tpu_custom_call" | custom-call | tf_op jit(solution)/shard_map/block/pallas_call | solution.py:427
  32.5 1.3 %hand_out.1 = (bf16[3,192,896]{2,1,0:T(8,128)(2,1)}, bf16[3,128,896]{2,1,0:T(8,128)(2,1)}, f32[112,224]{1,0:T(8,128)}) custom-call(bf16[3,192,896]{2,1,0:T(8,128)(2,1)S(1)} %get-tuple-element.9.home, bf16[3,128,896]{2,1,0:T(8,128)(2,1)S(1)} %get-tuple-element.10.box, f32[112,224]{1,0:T(8,128)S(1)} %get-tuple-element.11.weight), custom_call_target="tpu_custom_call" | custom-call | tf_op jit(solution)/shard_map/hand_out/pallas_call | solution.py:466

commit v7 on v6

--- a/solution.py
+++ b/solution.py
@@ -128,7 +128,7 @@
 
 F32 = jnp.float32
 BF16 = jnp.bfloat16
-EARLY = 5
+EARLY = 4
 CUT = 64
 
 
@@ -313,9 +313,11 @@
     started += [pass_a, pass_b]
     for copy in (w_c, pass_x, pass_y, pass_a, pass_b):
         copy.wait_recv()
-    backs[...] = dot(w_all[...], cot, (1, 1)).astype(BF16)
-    back_out[...] = dot(backs[:ahead], pick, (1, 0)).astype(BF16)
+    first = dot(w_all[:ahead], cot, (1, 1)).astype(BF16)
+    back_out[...] = dot(first, pick, (1, 0)).astype(BF16)
     ahead_back = e_push(3, back_out, back_in)
+    backs[:ahead] = first
+    backs[ahead:] = dot(w_all[ahead:], cot, (1, 1)).astype(BF16)
 
     def home_group(heads):
         rows = [pl.ds(h * pad, pad) for h in heads]

time: 34 us -> 34.8 us (1.024)
  Pallas kernels: 33.2 us -> 34 us
    pallas_call x1, Pallas kernels: 31.8 us -> 32.7 us  [fused(): pl.pallas_call(block_kernel, out_shape=tuple((pltpu.VMEM(each.shape, each...]
where the time goes in v7:
time: 34.8 us; the launch traced here: 34.6 us
  Pallas kernels  34 us (98%)
  between operations  0.64 us (2%)
    pallas_call x1, Pallas kernels, fused(): pl.pallas_call(block_kernel, out_shape=tuple((pltpu.VMEM(each.shape, each...  32.7 us
    pallas_call x1, Pallas kernels, fused(): pl.pallas_call(hand_out, out_shape=results, in_specs=[vmem] * 3, out_spec...  1.33 us

profile of v7, /device:TPU:0, one launch (start us, length us, event | category | flops | bytes accessed | tf_op | source)
XLA Modules:
  0.0 34.6 jit_solution(17210773872248040357)
XLA Ops:
  0.6 32.7 %block.1 = (bf16[3,192,896]{2,1,0:T(8,128)(2,1)S(1)}, bf16[3,128,896]{2,1,0:T(8,128)(2,1)S(1)}, f32[112,224]{1,0:T(8,128)S(1)}) custom-call(s32[3,1,4]{2,1,0:T(1,128)} %bitcast.13, s32[1,2,3]{2,1,0:T(2,128)} %moves_hbm.1, bf16[3,192,896]{2,1,0:T(8,128)(2,1)} %bitcast.11, bf16[192,896]{1,0:T(8,128)(2,1)} %bitcast.12, bf16[112,896]{1,0:T(8,128)(2,1)} %w_ref.1), custom_call_target="tpu_custom_call" | custom-call | tf_op jit(solution)/shard_map/block/pallas_call | solution.py:429
  33.3 1.3 %hand_out.1 = (bf16[3,192,896]{2,1,0:T(8,128)(2,1)}, bf16[3,128,896]{2,1,0:T(8,128)(2,1)}, f32[112,224]{1,0:T(8,128)}) custom-call(bf16[3,192,896]{2,1,0:T(8,128)(2,1)S(1)} %get-tuple-element.9.home, bf16[3,128,896]{2,1,0:T(8,128)(2,1)S(1)} %get-tuple-element.10.box, f32[112,224]{1,0:T(8,128)S(1)} %get-tuple-element.11.weight), custom_call_target="tpu_custom_call" | custom-call | tf_op jit(solution)/shard_map/hand_out/pallas_call | solution.py:468

commit v8 on v7

--- a/solution.py
+++ b/solution.py
@@ -128,7 +128,7 @@
 
 F32 = jnp.float32
 BF16 = jnp.bfloat16
-EARLY = 4
+EARLY = 5
 CUT = 64
 
 
@@ -240,9 +240,10 @@
         return copy
 
     early = []
+    near = -(-ahead // 128) * 128
     for i in range(3):
         fetches[2 + i].wait()
-        qkv_ref[i] = nat_ref[i].T
+        qkv_ref[i, :near] = nat_ref[i, :, :near].T
         early_out[i] = dot(qkv_ref[i, :ahead], pick, (1, 0)).astype(BF16)
         early.append(e_push(i, early_out.at[i], early_in.at[i]))
 
@@ -264,6 +265,8 @@
         ds = pf * (dp - jnp.sum(pf * dp, axis=0, keepdims=True))
         return (ds * HSIZE ** (-0.5)).astype(BF16)
 
+    for i in range(3):
+        qkv_ref[i, near:] = nat_ref[i, :, near:].T
     for fetch in fetches[5:]:
         fetch.wait()
     cot = g_ref[...]

time: 34.8 us -> 33.6 us (0.966)
  Pallas kernels: 34 us -> 32.9 us
    pallas_call x1, Pallas kernels: 32.7 us -> 31.5 us  [fused(): pl.pallas_call(block_kernel, out_shape=tuple((pltpu.VMEM(each.shape, each...]
where the time goes in v8:
time: 33.6 us; the launch traced here: 33.5 us
  Pallas kernels  32.9 us (98%)
  between operations  0.64 us (2%)
    pallas_call x1, Pallas kernels, fused(): pl.pallas_call(block_kernel, out_shape=tuple((pltpu.VMEM(each.shape, each...  31.5 us
    pallas_call x1, Pallas kernels, fused(): pl.pallas_call(hand_out, out_shape=results, in_specs=[vmem] * 3, out_spec...  1.33 us

profile of v8, /device:TPU:0, one launch (start us, length us, event | category | flops | bytes accessed | tf_op | source)
XLA Modules:
  0.0 33.5 jit_solution(5105511917957011412)
XLA Ops:
  0.6 31.5 %block.1 = (bf16[3,192,896]{2,1,0:T(8,128)(2,1)S(1)}, bf16[3,128,896]{2,1,0:T(8,128)(2,1)S(1)}, f32[112,224]{1,0:T(8,128)S(1)}) custom-call(s32[3,1,4]{2,1,0:T(1,128)} %bitcast.13, s32[1,2,3]{2,1,0:T(2,128)} %moves_hbm.1, bf16[3,192,896]{2,1,0:T(8,128)(2,1)} %bitcast.11, bf16[192,896]{1,0:T(8,128)(2,1)} %bitcast.12, bf16[112,896]{1,0:T(8,128)(2,1)} %w_ref.1), custom_call_target="tpu_custom_call" | custom-call | tf_op jit(solution)/shard_map/block/pallas_call | solution.py:432
  32.2 1.3 %hand_out.1 = (bf16[3,192,896]{2,1,0:T(8,128)(2,1)}, bf16[3,128,896]{2,1,0:T(8,128)(2,1)}, f32[112,224]{1,0:T(8,128)}) custom-call(bf16[3,192,896]{2,1,0:T(8,128)(2,1)S(1)} %get-tuple-element.9.home, bf16[3,128,896]{2,1,0:T(8,128)(2,1)S(1)} %get-tuple-element.10.box, f32[112,224]{1,0:T(8,128)S(1)} %get-tuple-element.11.weight), custom_call_target="tpu_custom_call" | custom-call | tf_op jit(solution)/shard_map/hand_out/pallas_call | solution.py:471
